TPU v7x, 256 devices: a whole 4x4x8 slice. The times are simulated.
256 devices in a mesh: box: 32 (over z, y), leaf: 8 (over x, core).
Axes of the slice: x: 4, y: 4, z: 8, core: 2. Of those that a mesh axis runs over, the one named last changes fastest.
Arguments:
- sources: bfloat16 [8, 216, 64, 4096], P('leaf', None, None, 'box'), may hold values from -6 to 6
- upward_maps: bfloat16 [8, 216, 216], replicated, may hold values from -0.15625 to 0.15625
- downward_maps: bfloat16 [8, 216, 216], replicated, may hold values from -0.3125 to 0.3125
- cross_maps: bfloat16 [16, 216, 216], replicated, may hold values from -0.1875 to 0.1875
- child_octant: int32 [8, 4096], P('leaf', 'box'), may hold values from 0 to 7
- child_parent: int32 [8, 4096], P('leaf', 'box'), may hold values from 0 to 15
- parent_box: int32 [8, 512], P('leaf', 'box'), may hold values from 0 to 127, as said below
- send_index: int32 [8, 32, 32, 4], P('leaf', 'box'), may hold values from 0 to 127
- near_source: int32 [8, 16, 512], P('leaf', None, 'box'), may hold values from 0 to 127
- near_target: int32 [8, 16, 512], P('leaf', None, 'box'), may hold values from 0 to 127
- far_source: int32 [8, 16, 512], P('leaf', None, 'box'), may hold values from 0 to 127
- far_target: int32 [8, 16, 512], P('leaf', None, 'box'), may hold values from 0 to 127
Outputs:
- expansion: bfloat16 [8, 216, 64, 4096], P('leaf', None, None, 'box')
Inputs may be any that keep to these rules, and one draw needn't show every extreme that they name: `parent_box`: within one level and one box device the 16 parent slots name distinct boxes.
All inputs are finite; a program needn't handle non-finite values.
Results may differ from a plain program's by a relative error of at most 0.0095.
Values may be sent and summed in bfloat16 or wider, within the bound.
A program may use at most 128 MiB of HBM per device.

v0:
```python
import jax
import jax.numpy as jnp
from jax import lax
from jax.sharding import PartitionSpec as P


def passed_along(block, axis, distance):
    devices = range(lax.axis_size(axis))
    route = [(i - distance, i) for i in devices if i - distance in devices]
    return lax.ppermute(block, axis, route)


def move_down(incoming, bucket_index, downward_maps, far_field):
    coeffs, vectors, parent_count = incoming.shape
    expanded = jnp.einsum(
        "opq,qwr->pwro", downward_maps, incoming, preferred_element_type=jnp.float32
    )
    expanded = expanded.reshape(coeffs, vectors, parent_count * 8)
    return (far_field + jnp.take(expanded, bucket_index, axis=2)).astype(jnp.bfloat16)


def translate_pairs(source_pool, pair_source, pair_target, cross_maps, box_count):
    rows_q, rows_w = (source_pool.shape[0], source_pool.shape[1])
    direction_count, per_pair = pair_source.shape
    group_size = max(1, min(direction_count, 2 * box_count // per_pair))
    total = jnp.zeros((rows_q, rows_w, box_count), jnp.float32)
    for start_dir in range(0, direction_count, group_size):
        group_maps = cross_maps[start_dir : start_dir + group_size]
        group_src = pair_source[start_dir : start_dir + group_size]
        group_dst = pair_target[start_dir : start_dir + group_size]
        group_count = group_maps.shape[0]
        gathered = jnp.take(source_pool, group_src.reshape(-1), axis=2).reshape(
            rows_q, rows_w, group_count, per_pair
        )
        moved = jnp.einsum(
            "kpq,qwkb->pwkb", group_maps, gathered, preferred_element_type=jnp.float32
        )
        total = total.at[:, :, group_dst.reshape(-1)].add(
            moved.reshape(rows_q, rows_w, group_count * per_pair)
        )
    return total


def per_device(
    sources,
    upward_maps,
    downward_maps,
    cross_maps,
    child_octant,
    child_parent,
    parent_box,
    send_index,
    near_source,
    near_target,
    far_source,
    far_target,
):
    leaf_count = lax.axis_size("leaf")
    coeffs, vectors, box_count = (sources.shape[1], sources.shape[2], sources.shape[3])
    parent_count = parent_box.shape[1]
    level_index = lax.axis_index("leaf")
    last_level = leaf_count - 1
    own_density = sources[0]
    parent_slots = parent_box[0]
    parents_here = child_parent[0]
    octants_here = child_octant[0]
    bucket_index = parents_here * 8 + octants_here
    slot_bucket = jnp.take(bucket_index, parent_slots)
    slot_octant = jnp.take(octants_here, parent_slots)
    slot_parent = jnp.take(parents_here, parent_slots)
    slot_row = slot_bucket // 8
    own_slots = jnp.take(own_density, parent_slots, axis=2).astype(jnp.float32)
    box_ids = jnp.arange(box_count, dtype=jnp.int32)
    in_slots = jnp.any(box_ids[:, None] == parent_slots[None, :], axis=1)
    kept_boxes = jnp.where(in_slots[None, None, :], 0.0, own_density.astype(jnp.float32))
    base_buckets = (
        jnp.zeros((coeffs, vectors, parent_count * 8), jnp.float32)
        .at[:, :, bucket_index]
        .add(kept_boxes)
    )
    base_rounded = base_buckets.astype(jnp.bfloat16)
    base_terms = jnp.einsum(
        "opq,qwro->pwr",
        upward_maps,
        base_rounded.reshape(coeffs, vectors, parent_count, 8),
        preferred_element_type=jnp.float32,
    )
    same_bucket = (slot_bucket[:, None] == slot_bucket[None, :]).astype(jnp.float32)
    slot_ids = jnp.arange(parent_count, dtype=jnp.int32)
    earlier_mask = (slot_ids[None, :] < slot_ids[:, None]).astype(jnp.float32)
    first_slot = (jnp.sum(same_bucket * earlier_mask, axis=1) == 0).astype(jnp.float32)
    base_at_slots = jnp.take(base_buckets, slot_bucket, axis=2)
    old_rounded = jnp.take(base_rounded, slot_bucket, axis=2).astype(jnp.float32)
    up_slot_maps = jnp.take(upward_maps, slot_octant, axis=0).astype(jnp.float32)
    incoming_up = jnp.zeros((coeffs, vectors, parent_count), jnp.bfloat16)
    for turn_index in range(leaf_count - 1):
        absorbed = (
            (own_slots + incoming_up.astype(jnp.float32)).astype(jnp.bfloat16).astype(jnp.float32)
        )
        fresh = base_at_slots + jnp.einsum(
            "jk,qwk->qwj", same_bucket, absorbed, precision=lax.Precision.HIGHEST
        )
        change = (fresh.astype(jnp.bfloat16).astype(jnp.float32) - old_rounded) * first_slot[
            None, None, :
        ]
        contribute_moved = jnp.einsum(
            "jpq,qwj->pwj", up_slot_maps, change, precision=lax.Precision.HIGHEST
        )
        sending = jnp.where(
            level_index == last_level - turn_index,
            base_terms.at[:, :, slot_row].add(contribute_moved).astype(jnp.bfloat16),
            jnp.zeros_like(incoming_up),
        )
        arrived = passed_along(sending, "leaf", -1)
        incoming_up = jnp.where(level_index == last_level - 1 - turn_index, arrived, incoming_up)
    absorbed_final = (own_slots + incoming_up.astype(jnp.float32)).astype(jnp.bfloat16)
    multipole = own_density.at[:, :, parent_slots].set(absorbed_final)
    outgoing = jnp.take(multipole, send_index.reshape(-1), axis=2)
    near_src = near_source[0]
    near_dst = near_target[0]
    far_src = far_source[0]
    far_dst = far_target[0]
    received = lax.all_to_all(outgoing, "box", split_axis=2, concat_axis=2, tiled=True)
    source_pool = jnp.concatenate([multipole, received], axis=2)
    pair_source = jnp.concatenate([near_src, far_src + box_count], axis=1)
    pair_target = jnp.concatenate([near_dst, far_dst], axis=1)
    far_field = translate_pairs(source_pool, pair_source, pair_target, cross_maps, box_count)
    far_at_slots = jnp.take(far_field, parent_slots, axis=2)
    down_slot_maps = jnp.take(downward_maps, slot_octant, axis=0)
    incoming_down = jnp.zeros((coeffs, vectors, parent_count), jnp.bfloat16)
    for turn_index in range(leaf_count - 1):
        parent_columns = jnp.take(incoming_down, slot_parent, axis=2)
        moved = jnp.einsum(
            "jpq,qwj->pwj", down_slot_maps, parent_columns, preferred_element_type=jnp.float32
        )
        sending = jnp.where(
            level_index == turn_index,
            (far_at_slots + moved).astype(jnp.bfloat16),
            jnp.zeros_like(incoming_down),
        )
        arrived = passed_along(sending, "leaf", 1)
        incoming_down = jnp.where(level_index == turn_index + 1, arrived, incoming_down)
    expansion = move_down(incoming_down, bucket_index, downward_maps, far_field)
    return expansion[None]


def solution(mesh):
    placed = (
        P("leaf", None, None, "box"),
        P(),
        P(),
        P(),
        P("leaf", "box"),
        P("leaf", "box"),
        P("leaf", "box"),
        P("leaf", "box", None, None),
        P("leaf", None, "box"),
        P("leaf", None, "box"),
        P("leaf", None, "box"),
        P("leaf", None, "box"),
    )
    return jax.shard_map(
        per_device,
        mesh=mesh,
        in_specs=placed,
        out_specs=P("leaf", None, None, "box"),
        check_vma=False,
    )
```

profile of v0, /device:TPU:1, one launch (start us, length us, event | category | flops | bytes accessed | tf_op | source)
XLA Modules:
  0.0 742.1 jit_solution(4106373223420692248)
XLA Ops:
  25.1 26.5 %scatter_fusion = f32[216,64,128]{0,1,2:T(8,128)} fusion(f32[216,64,128]{0,1,2:T(8,128)} %broadcast.222.clone, s32[128]{0:T(128)S(1)} %fusion.116, f32[128,216,64]{1,2,0:T(8,128)} %select_bitcast_fusion), kind=kCustom, calls=%fused_computation.20 | custom fusion | flops 1769472 | bytes 21234176 | tf_op jit(solution)/shard_map/scatter-add | solution.py:79
  118.5 8.9 %collective-permute-done.1 = bf16[216,64,16]{0,1,2:T(8,128)(2,1)} collective-permute-done((bf16[216,64,16]{0,1,2:T(8,128)(2,1)}, bf16[216,64,16]{0,1,2:T(8,128)(2,1)}, u32[]{:S(2)}, u32[]{:S(2)}) %collective-permute-start.1) | collective-permute-done | bytes 442400 | tf_op jit(solution)/shard_map/ppermute | solution.py:10
  141.8 8.5 %collective-permute-done.2 = bf16[216,64,16]{0,1,2:T(8,128)(2,1)} collective-permute-done((bf16[216,64,16]{0,1,2:T(8,128)(2,1)}, bf16[216,64,16]{0,1,2:T(8,128)(2,1)}, u32[]{:S(2)}, u32[]{:S(2)}) %collective-permute-start.2) | collective-permute-done | bytes 442400 | tf_op jit(solution)/shard_map/ppermute | solution.py:10
  164.8 8.9 %collective-permute-done.3 = bf16[216,64,16]{0,1,2:T(8,128)(2,1)} collective-permute-done((bf16[216,64,16]{0,1,2:T(8,128)(2,1)}, bf16[216,64,16]{0,1,2:T(8,128)(2,1)}, u32[]{:S(2)}, u32[]{:S(2)}) %collective-permute-start.3) | collective-permute-done | bytes 442400 | tf_op jit(solution)/shard_map/ppermute | solution.py:10
  188.8 8.7 %collective-permute-done.4 = bf16[216,64,16]{0,1,2:T(8,128)(2,1)} collective-permute-done((bf16[216,64,16]{0,1,2:T(8,128)(2,1)}, bf16[216,64,16]{0,1,2:T(8,128)(2,1)}, u32[]{:S(2)}, u32[]{:S(2)}) %collective-permute-start.4) | collective-permute-done | bytes 442400 | tf_op jit(solution)/shard_map/ppermute | solution.py:10
  213.7 8.5 %collective-permute-done.5 = bf16[216,64,16]{0,1,2:T(8,128)(2,1)} collective-permute-done((bf16[216,64,16]{0,1,2:T(8,128)(2,1)}, bf16[216,64,16]{0,1,2:T(8,128)(2,1)}, u32[]{:S(2)}, u32[]{:S(2)}) %collective-permute-start.5) | collective-permute-done | bytes 442400 | tf_op jit(solution)/shard_map/ppermute | solution.py:10
  236.4 8.5 %collective-permute-done.6 = bf16[216,64,16]{0,1,2:T(8,128)(2,1)S(1)} collective-permute-done((bf16[216,64,16]{0,1,2:T(8,128)(2,1)S(1)}, bf16[216,64,16]{0,1,2:T(8,128)(2,1)S(1)}, u32[]{:S(2)}, u32[]{:S(2)}) %collective-permute-start.6) | collective-permute-done | bytes 442400 | tf_op jit(solution)/shard_map/ppermute | solution.py:10
  258.6 11.9 %all-to-all-start = ((bf16[216,64,128]{0,1,2:T(8,128)(2,1)}), bf16[216,64,128]{0,1,2:T(8,128)(2,1)}, u32[]{:S(2)}, u32[]{:S(2)}) async-start(bf16[216,64,128]{0,1,2:T(8,128)(2,1)} %select_bitcast_fusion.1), calls=%async_computation | async-start | bytes 8388608 | tf_op jit(solution)/shard_map/all_to_all | solution.py:123
  278.3 81.5 %all-to-all-done = bf16[216,64,128]{0,1,2:T(8,128)(2,1)} async-done(((bf16[216,64,128]{0,1,2:T(8,128)(2,1)}), bf16[216,64,128]{0,1,2:T(8,128)(2,1)}, u32[]{:S(2)}, u32[]{:S(2)}) %all-to-all-start) | async-done | bytes 3538976 | tf_op jit(solution)/shard_map/all_to_all | solution.py:123
  364.5 12.0 %gather_fusion.8 = bf16[256,216,64]{1,2,0:T(8,128)(2,1)} fusion(bf16[216,64,256]{0,1,2:T(8,128)(2,1)} %constant_dynamic-update-slice_fusion, s32[1024]{0:T(1024)S(1)} %get-tuple-element.35), kind=kCustom, calls=%fused_computation.4.clone | custom fusion | bytes 14156800 | tf_op jit(solution)/shard_map/jit(_take)/gather | solution.py:32
  376.5 7.4 broadcast_select_fusion.1
  383.9 14.9 %convolution_bitcast_fusion.1 = f32[216,64,8,32]{0,3,1,2:T(8,128)} fusion(bf16[216,64,8,32]{0,1,3,2:T(8,128)(2,1)} %bitcast.226, bf16[16,216,216]{2,1,0:T(8,128)(2,1)} %param.27), kind=kOutput, calls=%fused_computation.32 | convolution fusion | flops 1528823808 | bytes 23429120 | tf_op jit(solution)/shard_map/kpq,qwkb->pwkb/dot_general | solution.py:35
  405.4 20.5 %copy.97 = f32[256,216,64]{1,2,0:T(8,128)} copy(f32[256,216,64]{1,0,2:T(8,128)S(1)} %bitcast.224) | data formatting | bytes 28311552 | tf_op jit(solution)/shard_map/reshape | solution.py:39
  425.8 12.1 %gather_fusion.9 = bf16[256,216,64]{1,2,0:T(8,128)(2,1)} fusion(bf16[216,64,256]{0,1,2:T(8,128)(2,1)} %constant_dynamic-update-slice_fusion, s32[1024]{0:T(1024)S(1)} %get-tuple-element.34), kind=kCustom, calls=%fused_computation.11.clone | custom fusion | bytes 14156800 | tf_op jit(solution)/shard_map/jit(_take)/gather | solution.py:32
  438.0 7.4 broadcast_select_fusion
  445.4 14.9 %convolution_bitcast_fusion = f32[216,64,8,32]{0,3,1,2:T(8,128)} fusion(bf16[216,64,8,32]{0,1,3,2:T(8,128)(2,1)} %bitcast.227, bf16[16,216,216]{2,1,0:T(8,128)(2,1)} %param.27), kind=kOutput, calls=%fused_computation.31 | convolution fusion | flops 1528823808 | bytes 23429120 | tf_op jit(solution)/shard_map/kpq,qwkb->pwkb/dot_general | solution.py:35
  466.9 20.1 %copy.100 = f32[256,216,64]{1,2,0:T(8,128)} copy(f32[256,216,64]{1,0,2:T(8,128)S(1)} %bitcast.225) | data formatting | bytes 28311552 | tf_op jit(solution)/shard_map/reshape | solution.py:39
  491.2 51.9 %scatter_fusion.9 = f32[216,64,128]{0,1,2:T(8,128)} fusion(f32[216,64,128]{0,1,2:T(8,128)} %broadcast.222, s32[256]{0:T(256)S(1)} %bitcast.234, f32[256,216,64]{1,2,0:T(8,128)} %copy.97), kind=kCustom, calls=%fused_computation.29 | custom fusion | flops 3538944 | bytes 42468352 | tf_op jit(solution)/shard_map/scatter-add | solution.py:38
  543.1 51.9 %scatter_fusion.10 = f32[216,64,128]{0,1,2:T(8,128)} fusion(f32[216,64,128]{0,1,2:T(8,128)} %scatter_fusion.9, s32[256]{0:T(256)S(1)} %bitcast.233, f32[256,216,64]{1,2,0:T(8,128)} %copy.100), kind=kCustom, calls=%fused_computation.30 | custom fusion | flops 3538944 | bytes 42468352 | tf_op jit(solution)/shard_map/scatter-add | solution.py:38
  601.3 12.7 %collective-permute-start.7 = (bf16[216,64,16]{0,1,2:T(8,128)(2,1)S(1)}, bf16[216,64,16]{0,1,2:T(8,128)(2,1)S(1)}, u32[]{:S(2)}, u32[]{:S(2)}) collective-permute-start(bf16[216,64,16]{0,1,2:T(8,128)(2,1)S(1)} %fusion.39), channel_id=1, source_target_pairs={{0,1},{1,2},{2,3},{3,4},{4,5},{5,6},{6,7},{8,9},{9,10},{10,11},{11... | collective-permute-start | bytes 1327112 | tf_op jit(solution)/shard_map/ppermute | solution.py:10
  701.9 8.1 %copy.176 = f32[216,64,16,8]{0,3,2,1:T(8,128)S(1)} copy(f32[216,64,16,8]{0,2,3,1:T(8,128)S(1)} %convolution_bitcast_fusion.2) | data formatting | bytes 14155776 | tf_op jit(solution)/shard_map/opq,qwr->pwro/transpose | solution.py:15
  710.0 8.3 %copy.103 = f32[216,64,128]{0,1,2:T(8,128)} copy(f32[216,64,128]{0,2,1:T(8,128)S(1)} %bitcast.228) | data formatting | bytes 14155776 | tf_op jit(solution)/shard_map/reshape | solution.py:18
  718.3 7.7 %gather_fusion.1 = f32[128,216,64]{1,2,0:T(8,128)} fusion(f32[216,64,128]{0,1,2:T(8,128)} %copy.103, s32[1024]{0:T(1024)S(1)} %get-tuple-element.32), kind=kCustom, calls=%fused_computation.19 | custom fusion | bytes 14156288 | tf_op jit(solution)/shard_map/jit(_take)/gather | solution.py:19
  726.0 8.5 %fusion.3 = bf16[1,216,64,128]{1,2,3,0:T(8,128)(2,1)} fusion(f32[216,64,128]{0,1,2:T(8,128)} %scatter_fusion.10, f32[128,216,64]{1,2,0:T(8,128)} %gather_fusion.1, pred[128]{0:T(512)(128)(4,1)S(1)} %copy-done.8), kind=kLoop, calls=%fused_computation.41 | loop fusion | flops 5308416 | bytes 17694848 | tf_op jit(solution)/shard_map/broadcast_in_dim | solution.py:144
  (166 shorter events, 310.7 us)
Async XLA Ops:
  0.0 271.0 %copy-start = (bf16[8,216,216]{2,1,0:T(8,128)(2,1)S(1)}, bf16[8,216,216]{2,1,0:T(8,128)(2,1)}, u32[]{:S(2)}) copy-start(bf16[8,216,216]{2,1,0:T(8,128)(2,1)} %param.26) | copy-start | bytes 2239492
  5.8 8.9 %copy-start.10 = (s32[1,16]{1,0:T(1,128)S(1)}, s32[1,16]{1,0:T(1,128)}, u32[]{:S(2)}) copy-start(s32[1,16]{1,0:T(1,128)} %param.30) | copy-start | bytes 196
  93.0 11.7 %collective-permute-start = (bf16[216,64,16]{0,1,2:T(8,128)(2,1)}, bf16[216,64,16]{0,1,2:T(8,128)(2,1)}, u32[]{:S(2)}, u32[]{:S(2)}) collective-permute-start(bf16[216,64,16]{0,1,2:T(8,128)(2,1)} %convert_select_fusion.6), channel_id=1, source_target_pairs={{1,0},{2,1},{3,2},{4,3},{5,4},{6,5},{7,6},{9,8},{10,9},{11,10},{12... | collective-permute-start | bytes 1327112 | tf_op jit(solution)/shard_map/ppermute | solution.py:10
  116.6 10.8 %collective-permute-start.1 = (bf16[216,64,16]{0,1,2:T(8,128)(2,1)}, bf16[216,64,16]{0,1,2:T(8,128)(2,1)}, u32[]{:S(2)}, u32[]{:S(2)}) collective-permute-start(bf16[216,64,16]{0,1,2:T(8,128)(2,1)} %convert_select_fusion.5), channel_id=1, source_target_pairs={{1,0},{2,1},{3,2},{4,3},{5,4},{6,5},{7,6},{9,8},{10,9},{11,10},{12... | collective-permute-start | bytes 1327112 | tf_op jit(solution)/shard_map/ppermute | solution.py:10
  139.4 10.8 %collective-permute-start.2 = (bf16[216,64,16]{0,1,2:T(8,128)(2,1)}, bf16[216,64,16]{0,1,2:T(8,128)(2,1)}, u32[]{:S(2)}, u32[]{:S(2)}) collective-permute-start(bf16[216,64,16]{0,1,2:T(8,128)(2,1)} %convert_select_fusion.4), channel_id=1, source_target_pairs={{1,0},{2,1},{3,2},{4,3},{5,4},{6,5},{7,6},{9,8},{10,9},{11,10},{12... | collective-permute-start | bytes 1327112 | tf_op jit(solution)/shard_map/ppermute | solution.py:10
  162.9 10.8 %collective-permute-start.3 = (bf16[216,64,16]{0,1,2:T(8,128)(2,1)}, bf16[216,64,16]{0,1,2:T(8,128)(2,1)}, u32[]{:S(2)}, u32[]{:S(2)}) collective-permute-start(bf16[216,64,16]{0,1,2:T(8,128)(2,1)} %convert_select_fusion.3), channel_id=1, source_target_pairs={{1,0},{2,1},{3,2},{4,3},{5,4},{6,5},{7,6},{9,8},{10,9},{11,10},{12... | collective-permute-start | bytes 1327112 | tf_op jit(solution)/shard_map/ppermute | solution.py:10
  186.7 10.8 %collective-permute-start.4 = (bf16[216,64,16]{0,1,2:T(8,128)(2,1)}, bf16[216,64,16]{0,1,2:T(8,128)(2,1)}, u32[]{:S(2)}, u32[]{:S(2)}) collective-permute-start(bf16[216,64,16]{0,1,2:T(8,128)(2,1)} %convert_select_fusion.2), channel_id=1, source_target_pairs={{1,0},{2,1},{3,2},{4,3},{5,4},{6,5},{7,6},{9,8},{10,9},{11,10},{12... | collective-permute-start | bytes 1327112 | tf_op jit(solution)/shard_map/ppermute | solution.py:10
  202.4 10.9 %copy-start.9 = (s32[1,1,32,4]{2,3,1,0:T(4,128)S(1)}, s32[1,1,32,4]{2,3,1,0:T(4,128)}, u32[]{:S(2)}) copy-start(s32[1,1,32,4]{2,3,1,0:T(4,128)} %param.31) | copy-start | bytes 1540
  211.5 10.8 %collective-permute-start.5 = (bf16[216,64,16]{0,1,2:T(8,128)(2,1)}, bf16[216,64,16]{0,1,2:T(8,128)(2,1)}, u32[]{:S(2)}, u32[]{:S(2)}) collective-permute-start(bf16[216,64,16]{0,1,2:T(8,128)(2,1)} %convert_select_fusion.1), channel_id=1, source_target_pairs={{1,0},{2,1},{3,2},{4,3},{5,4},{6,5},{7,6},{9,8},{10,9},{11,10},{12... | collective-permute-start | bytes 1327112 | tf_op jit(solution)/shard_map/ppermute | solution.py:10
  229.4 15.5 %copy-start.2 = (bf16[216,64,16]{0,1,2:T(8,128)(2,1)S(1)}, bf16[216,64,16]{0,1,2:T(8,128)(2,1)}, u32[]{:S(2)}) copy-start(bf16[216,64,16]{0,1,2:T(8,128)(2,1)} %get-tuple-element.17) | copy-start | bytes 1327108
  234.4 10.5 %collective-permute-start.6 = (bf16[216,64,16]{0,1,2:T(8,128)(2,1)S(1)}, bf16[216,64,16]{0,1,2:T(8,128)(2,1)S(1)}, u32[]{:S(2)}, u32[]{:S(2)}) collective-permute-start(bf16[216,64,16]{0,1,2:T(8,128)(2,1)S(1)} %convert_select_fusion), channel_id=1, source_target_pairs={{1,0},{2,1},{3,2},{4,3},{5,4},{6,5},{7,6},{9,8},{10,9},{11,10},{12... | collective-permute-start | bytes 1327112 | tf_op jit(solution)/shard_map/ppermute | solution.py:10
  258.5 11.9 %copy-start.7 = (s32[1,16,16]{2,1,0:T(8,128)S(1)}, s32[1,16,16]{2,1,0:T(8,128)}, u32[]{:S(2)}) copy-start(s32[1,16,16]{2,1,0:T(8,128)} %param.34) | copy-start | bytes 3076
  258.5 12.0 %copy-start.4 = (s32[1,16,16]{2,1,0:T(8,128)S(1)}, s32[1,16,16]{2,1,0:T(8,128)}, u32[]{:S(2)}) copy-start(s32[1,16,16]{2,1,0:T(8,128)} %param.32) | copy-start | bytes 3076
  258.5 12.2 %copy-start.5 = (s32[1,16,16]{2,1,0:T(8,128)S(1)}, s32[1,16,16]{2,1,0:T(8,128)}, u32[]{:S(2)}) copy-start(s32[1,16,16]{2,1,0:T(8,128)} %param.35) | copy-start | bytes 3076
  258.5 12.2 %copy-start.6 = (s32[1,16,16]{2,1,0:T(8,128)S(1)}, s32[1,16,16]{2,1,0:T(8,128)}, u32[]{:S(2)}) copy-start(s32[1,16,16]{2,1,0:T(8,128)} %param.33) | copy-start | bytes 3076
  258.6 101.2 %all-to-all-start = ((bf16[216,64,128]{0,1,2:T(8,128)(2,1)}), bf16[216,64,128]{0,1,2:T(8,128)(2,1)}, u32[]{:S(2)}, u32[]{:S(2)}) async-start(bf16[216,64,128]{0,1,2:T(8,128)(2,1)} %select_bitcast_fusion.1), calls=%async_computation | async-start | bytes 8388608 | tf_op jit(solution)/shard_map/all_to_all | solution.py:123
  601.3 18.8 %collective-permute-start.7 = (bf16[216,64,16]{0,1,2:T(8,128)(2,1)S(1)}, bf16[216,64,16]{0,1,2:T(8,128)(2,1)S(1)}, u32[]{:S(2)}, u32[]{:S(2)}) collective-permute-start(bf16[216,64,16]{0,1,2:T(8,128)(2,1)S(1)} %fusion.39), channel_id=1, source_target_pairs={{0,1},{1,2},{2,3},{3,4},{4,5},{5,6},{6,7},{8,9},{9,10},{10,11},{11... | collective-permute-start | bytes 1327112 | tf_op jit(solution)/shard_map/ppermute | solution.py:10
  623.0 10.5 %collective-permute-start.8 = (bf16[216,64,16]{0,1,2:T(8,128)(2,1)S(1)}, bf16[216,64,16]{0,1,2:T(8,128)(2,1)S(1)}, u32[]{:S(2)}, u32[]{:S(2)}) collective-permute-start(bf16[216,64,16]{0,1,2:T(8,128)(2,1)S(1)} %fusion.40), channel_id=1, source_target_pairs={{0,1},{1,2},{2,3},{3,4},{4,5},{5,6},{6,7},{8,9},{9,10},{10,11},{11... | collective-permute-start | bytes 1327112 | tf_op jit(solution)/shard_map/ppermute | solution.py:10
  636.4 10.5 %collective-permute-start.9 = (bf16[216,64,16]{0,1,2:T(8,128)(2,1)S(1)}, bf16[216,64,16]{0,1,2:T(8,128)(2,1)S(1)}, u32[]{:S(2)}, u32[]{:S(2)}) collective-permute-start(bf16[216,64,16]{0,1,2:T(8,128)(2,1)S(1)} %fusion.41), channel_id=1, source_target_pairs={{0,1},{1,2},{2,3},{3,4},{4,5},{5,6},{6,7},{8,9},{9,10},{10,11},{11... | collective-permute-start | bytes 1327112 | tf_op jit(solution)/shard_map/ppermute | solution.py:10
  649.8 10.5 %collective-permute-start.10 = (bf16[216,64,16]{0,1,2:T(8,128)(2,1)S(1)}, bf16[216,64,16]{0,1,2:T(8,128)(2,1)S(1)}, u32[]{:S(2)}, u32[]{:S(2)}) collective-permute-start(bf16[216,64,16]{0,1,2:T(8,128)(2,1)S(1)} %fusion.42), channel_id=1, source_target_pairs={{0,1},{1,2},{2,3},{3,4},{4,5},{5,6},{6,7},{8,9},{9,10},{10,11},{11... | collective-permute-start | bytes 1327112 | tf_op jit(solution)/shard_map/ppermute | solution.py:10
  663.2 10.5 %collective-permute-start.11 = (bf16[216,64,16]{0,1,2:T(8,128)(2,1)S(1)}, bf16[216,64,16]{0,1,2:T(8,128)(2,1)S(1)}, u32[]{:S(2)}, u32[]{:S(2)}) collective-permute-start(bf16[216,64,16]{0,1,2:T(8,128)(2,1)S(1)} %fusion.43), channel_id=1, source_target_pairs={{0,1},{1,2},{2,3},{3,4},{4,5},{5,6},{6,7},{8,9},{9,10},{10,11},{11... | collective-permute-start | bytes 1327112 | tf_op jit(solution)/shard_map/ppermute | solution.py:10
  676.5 10.5 %collective-permute-start.12 = (bf16[216,64,16]{0,1,2:T(8,128)(2,1)S(1)}, bf16[216,64,16]{0,1,2:T(8,128)(2,1)S(1)}, u32[]{:S(2)}, u32[]{:S(2)}) collective-permute-start(bf16[216,64,16]{0,1,2:T(8,128)(2,1)S(1)} %fusion.44), channel_id=1, source_target_pairs={{0,1},{1,2},{2,3},{3,4},{4,5},{5,6},{6,7},{8,9},{9,10},{10,11},{11... | collective-permute-start | bytes 1327112 | tf_op jit(solution)/shard_map/ppermute | solution.py:10
  689.9 10.5 %collective-permute-start.13 = (bf16[216,64,16]{0,1,2:T(8,128)(2,1)S(1)}, bf16[216,64,16]{0,1,2:T(8,128)(2,1)S(1)}, u32[]{:S(2)}, u32[]{:S(2)}) collective-permute-start(bf16[216,64,16]{0,1,2:T(8,128)(2,1)S(1)} %fusion.45), channel_id=1, source_target_pairs={{0,1},{1,2},{2,3},{3,4},{4,5},{5,6},{6,7},{8,9},{9,10},{10,11},{11... | collective-permute-start | bytes 1327112 | tf_op jit(solution)/shard_map/ppermute | solution.py:10
  718.3 7.7 %copy-start.8 = (pred[128]{0:T(512)(128)(4,1)S(1)}, pred[128]{0:T(512)(128)(4,1)}, u32[]{:S(2)}) copy-start(pred[128]{0:T(512)(128)(4,1)} %get-tuple-element.6) | copy-start | bytes 388
  (3 other events, 12.6 us)
where the time goes:
time: 753 us; the launch traced here: 742 us
  other arithmetic  224 us (30%)
  waiting for transfers between devices  183 us (24%)
  local copies, waits for them, and re-layouts  175 us (23%)
  matrix products  91.2 us (12%)
  starting transfers between devices  68.3 us (9%)
    scatter-add x2, other arithmetic, translate_pairs(): total.at[:, :, group_dst.reshape(-1)]  104 us
    ppermute x14, waiting for transfers between devices, passed_along(): return lax.ppermute(block, axis, route)  101 us
    all_to_all x1, waiting for transfers between devices, per_device(): lax.all_to_all(outgoing, 'box', split_axis=2, concat_axis=2, tiled=True)  81.5 us
    ppermute x14, starting transfers between devices, passed_along(): return lax.ppermute(block, axis, route)  56.4 us
    reshape x2, local copies, waits for them, and re-layouts, translate_pairs(): moved.reshape(rows_q, rows_w, group_count * per_pair)  40.5 us
    dot_general x2, matrix products, translate_pairs(): jnp.einsum('kpq,qwkb->pwkb', group_maps, gathered, preferred_element_type...  29.8 us
    scatter-add x1, other arithmetic, per_device(): base_buckets = jnp.zeros((coeffs, vectors, parent_count * 8), jnp.float32...  26.5 us
    scatter-add x7, other arithmetic, per_device(): base_terms.at[:, :, slot_row].add(contribute_moved).astype(jnp.bfloat16)  26.1 us
  transfers between devices with their start and end apart: 15, of which 15 were waited for; matrix products, arithmetic and copies ran while one was open for 1% of the time, Pallas kernels for 0%

commit v1 on v0

v1 whole, which is shorter than its diff:
```python
import functools

import jax
import jax.numpy as jnp
from jax import lax
from jax.experimental import pallas as pl
from jax.experimental.pallas import tpu as pltpu
from jax.sharding import PartitionSpec as P

BF = jnp.bfloat16
F32 = jnp.float32
MESH = pl.DeviceIdType.MESH
QP = 256
CAP = 4


def dot_nn(a, b):
    return lax.dot_general(a, b, (((1,), (0,)), ((), ())), preferred_element_type=F32)


def dot_nt(a, b):
    return lax.dot_general(a, b, (((1,), (1,)), ((), ())), preferred_element_type=F32)


def iota(shape, dim):
    return lax.broadcasted_iota(jnp.int32, shape, dim)


def onehot(mask):
    return mask.astype(F32).astype(BF)


def column_of(table, by_column):
    a, b = table.shape
    n = a * b
    row = iota((n, 1), 0)
    of_a, of_b = (row % a, row // a) if by_column else (row // b, row % b)
    picked = dot_nn(onehot(of_a == iota((n, a), 1)), table.astype(F32).astype(BF))
    return jnp.sum(jnp.where(of_b == iota((n, b), 1), picked, 0.0), axis=1, keepdims=True)


def is_at(column, width):
    return onehot(column == iota((column.shape[0], width), 1).astype(F32))


def kernel(
    dims,
    x_ref, up_ref, down_ref, cross_ref, octant_ref, parent_ref, slots_ref,
    send_index_ref, near_src_ref, near_dst_ref, far_src_ref, far_dst_ref,
    out_ref,
    maps, x32, m_buf, bucket, cin, cout, st, send, recv, gath, moved, far, ein, eout, shift, ost,
    sem_cs, sem_cr, sem_es, sem_er, sem_as, sem_ar, sem_own,
):
    nbox, nleaf, q, w_all, boxes, par, wc, rows_k = dims
    chunks = w_all // wc
    me = lax.axis_index("box")
    level = lax.axis_index("leaf")
    last = nleaf - 1

    barrier = pltpu.get_barrier_semaphore()

    def greet(j, carry):
        pl.semaphore_signal(barrier, inc=1, device_id={"box": lax.rem(me + j, nbox)}, device_id_type=MESH)
        return carry

    lax.fori_loop(1, nbox, greet, 0)

    @pl.when(level > 0)
    def _():
        pl.semaphore_signal(barrier, inc=1, device_id={"leaf": level - 1}, device_id_type=MESH)

    @pl.when(level < last)
    def _():
        pl.semaphore_signal(barrier, inc=1, device_id={"leaf": level + 1}, device_id_type=MESH)

    eye = onehot(iota((boxes, boxes), 0) == iota((boxes, boxes), 1))
    bucket_row = octant_ref[...] * par + parent_ref[...]
    oh_bucket = onehot(bucket_row == iota((8 * par, boxes), 0))
    slot_col = column_of(slots_ref[...], False)
    oh_slot = is_at(slot_col, boxes)
    oh_slot_t = onehot(slots_ref[...] == iota((boxes, par), 0))
    bucket_col = column_of(bucket_row, False)
    oh_bucket_t = is_at(bucket_col, 8 * par)
    oh_send = is_at(column_of(send_index_ref[...], True), boxes)
    oh_near_src = is_at(column_of(near_src_ref[...], False), boxes)
    far_src = far_src_ref[...]
    oh_far_src = is_at(column_of((far_src % CAP) * nbox + far_src // CAP, False), CAP * nbox)
    near_dst_col = column_of(near_dst_ref[...], False)
    far_dst_col = column_of(far_dst_ref[...], False)
    oh_near_dst = is_at(near_dst_col, boxes).astype(F32).T.astype(BF)
    oh_far_dst = is_at(far_dst_col, boxes).astype(F32).T.astype(BF)

    n_up, n_down, n_cross = up_ref.shape[0], down_ref.shape[0], cross_ref.shape[0]

    def pad_maps(source, base, count):
        def one(k, carry):
            maps[base + k] = jnp.zeros((QP, QP), BF)
            maps[base + k, 0:q, 0:q] = source[k]
            return carry
        lax.fori_loop(0, count, one, 0)

    pad_maps(up_ref, 0, n_up)
    pad_maps(down_ref, n_up, n_down)
    pad_maps(cross_ref, n_up + n_down, n_cross)

    x32[q * 16 :, :] = jnp.zeros(((QP - q) * 16, boxes), F32)

    def turn(g, carry):
        x32[0 : q * 16, :] = (
            x_ref[:, pl.ds(pl.multiple_of(g * 16, 16), 16), :].astype(F32).reshape(q * 16, boxes)
        )

        def one(w, inner):
            x_w = x32[pl.ds(w, QP, stride=16), :].astype(BF)
            m_buf[g * 16 + w] = dot_nt(eye, x_w).astype(BF)
            return inner

        lax.fori_loop(0, 16, one, 0, unroll=4)
        return carry

    lax.fori_loop(0, w_all // 16, turn, 0)

    @pl.when(level == last)
    def _():
        cin[...] = jnp.zeros_like(cin)

    @pl.when(level == 0)
    def _():
        ein[...] = jnp.zeros_like(ein)

    pl.semaphore_wait(
        barrier, nbox + 1 - (level == 0).astype(jnp.int32) - (level == last).astype(jnp.int32)
    )

    def chain(buf_from, buf_to, c, s_sem, r_sem, target):
        return pltpu.make_async_remote_copy(
            src_ref=buf_from.at[c], dst_ref=buf_to.at[c], send_sem=s_sem.at[c], recv_sem=r_sem.at[c],
            device_id={"leaf": target}, device_id_type=MESH,
        )

    def upward(c):
        return chain(cout, cin, c, sem_cs, sem_cr, jnp.maximum(level - 1, 0))

    def downward(c):
        return chain(eout, ein, c, sem_es, sem_er, jnp.minimum(level + 1, last))

    def exchange(c, j):
        to = lax.rem(me + j, nbox)
        return pltpu.make_async_remote_copy(
            src_ref=send.at[c, to], dst_ref=recv.at[c, me], send_sem=sem_as.at[c, j],
            recv_sem=sem_ar.at[c, j], device_id={"box": to}, device_id_type=MESH,
        )

    def from_peer(c, j):
        peer = lax.rem(me + nbox - j, nbox)
        return pltpu.make_async_remote_copy(
            src_ref=send.at[c, peer], dst_ref=recv.at[c, peer], send_sem=sem_as.at[c, j],
            recv_sem=sem_ar.at[c, j], device_id={"box": peer}, device_id_type=MESH,
        )

    def own_copy(c):
        return pltpu.make_async_copy(send.at[c, me], recv.at[c, me], sem_own.at[c])

    def up_step(c, carry):
        @pl.when(level < last)
        def _():
            upward(c).wait_recv()

        def merge(w, inner):
            at = c * wc + w
            m_w = (m_buf[at].astype(F32) + dot_nn(oh_slot_t, cin[c, w])).astype(BF)
            m_buf[at] = m_w
            bucket[w] = dot_nn(oh_bucket, m_w).astype(BF)
            return inner

        lax.fori_loop(0, wc, merge, 0, unroll=4)
        total = jnp.zeros((wc * par, QP), F32)
        for o in range(8):
            total += dot_nt(bucket[:, o * par : (o + 1) * par, :].reshape(wc * par, QP), maps[o])
        cout[c] = total.astype(BF).reshape(wc, par, QP)

        @pl.when(level > 0)
        def _():
            upward(c).start()

        def listed(w, inner):
            o_w = dot_nn(oh_send, m_buf[c * wc + w])
            for i in range(CAP):
                for h in range(2):
                    st[h, pl.ds(i * wc + w, nbox, stride=CAP * wc), :] = o_w[
                        i * nbox : (i + 1) * nbox, h * 128 : (h + 1) * 128
                    ]
            return inner

        lax.fori_loop(0, wc, listed, 0, unroll=4)
        for h in range(2):
            send[c, :, :, h * 128 : (h + 1) * 128] = st[h].astype(BF).reshape(nbox, CAP * wc, 128)

        def go(j, inner):
            exchange(c, j).start()
            return inner

        lax.fori_loop(1, nbox, go, 0)
        own_copy(c).start()
        return carry

    lax.fori_loop(0, chunks, up_step, 0)

    def apply_cross():
        def one(k, inner):
            at = pl.multiple_of(k * rows_k, 16)
            moved[:, pl.ds(at, rows_k), :] = (
                dot_nt(gath[:, pl.ds(at, rows_k), :].reshape(wc * rows_k, QP), maps[n_up + n_down + k])
                .astype(BF)
                .reshape(wc, rows_k, QP)
            )
            return inner

        lax.fori_loop(0, n_cross, one, 0, unroll=2)

    def down_step(c, carry):
        def near(w, inner):
            gath[w] = dot_nn(oh_near_src, m_buf[c * wc + w]).astype(BF)
            return inner

        lax.fori_loop(0, wc, near, 0, unroll=4)
        apply_cross()

        def near_add(w, inner):
            far[w] = dot_nn(oh_near_dst, moved[w])
            return inner

        lax.fori_loop(0, wc, near_add, 0, unroll=4)

        def arrived(j, inner):
            from_peer(c, j).wait_recv()
            return inner

        lax.fori_loop(1, nbox, arrived, 0)
        own_copy(c).wait()
        for h in range(2):
            st[h] = recv[c, :, :, h * 128 : (h + 1) * 128].astype(F32).reshape(nbox * CAP * wc, 128)

        def remote(w, inner):
            parts = []
            for i in range(CAP):
                parts.append(
                    jnp.concatenate(
                        [st[h, pl.ds(i * wc + w, nbox, stride=CAP * wc), :] for h in range(2)], axis=1
                    )
                )
            gath[w] = dot_nn(oh_far_src, jnp.concatenate(parts, axis=0).astype(BF)).astype(BF)
            return inner

        lax.fori_loop(0, wc, remote, 0, unroll=4)
        apply_cross()

        def far_add(w, inner):
            far[w] += dot_nn(oh_far_dst, moved[w])
            return inner

        lax.fori_loop(0, wc, far_add, 0, unroll=4)

        @pl.when(level > 0)
        def _():
            downward(c).wait_recv()

        for o in range(8):
            shift[:, o * par : (o + 1) * par, :] = (
                dot_nt(ein[c].reshape(wc * par, QP), maps[n_up + o]).astype(BF).reshape(wc, par, QP)
            )

        def expand(w, inner):
            e_w = (far[w] + dot_nn(oh_bucket_t, shift[w])).astype(BF)
            gath[w, 0:boxes, :] = e_w
            eout[c, w] = dot_nn(oh_slot, e_w).astype(BF)
            return inner

        lax.fori_loop(0, wc, expand, 0, unroll=4)

        @pl.when(level < last)
        def _():
            downward(c).start()

        def back(w, inner):
            e_t = gath[w, 0:boxes, :].astype(F32).T
            ost[pl.ds(lax.rem(c * wc, 16) + w, q, stride=16), :] = e_t[0:q, :]
            return inner

        lax.fori_loop(0, wc, back, 0, unroll=2)

        @pl.when(lax.rem((c + 1) * wc, 16) == 0)
        def _():
            out_ref[:, pl.ds(pl.multiple_of((c * wc) // 16 * 16, 16), 16), :] = (
                ost[...].reshape(q, 16, boxes).astype(BF)
            )

        return carry

    lax.fori_loop(0, chunks, down_step, 0)

    def finish(c, carry):
        def sent(j, inner):
            exchange(c, j).wait_send()
            return inner

        lax.fori_loop(1, nbox, sent, 0)

        @pl.when(level > 0)
        def _():
            upward(c).wait_send()

        @pl.when(level < last)
        def _():
            downward(c).wait_send()

        return carry

    lax.fori_loop(0, chunks, finish, 0)


def per_device(
    sources, upward_maps, downward_maps, cross_maps, child_octant, child_parent, parent_box,
    send_index, near_source, near_target, far_source, far_target,
):
    nbox, nleaf = lax.axis_size("box"), lax.axis_size("leaf")
    _, q, w_all, boxes = sources.shape
    par = parent_box.shape[1]
    rows_k = near_source.shape[2]
    pairs = near_source.shape[1] * rows_k
    wc = 16
    chunks = w_all // wc
    dims = (nbox, nleaf, q, w_all, boxes, par, wc, rows_k)
    n_maps = upward_maps.shape[0] + downward_maps.shape[0] + cross_maps.shape[0]
    dma = pltpu.SemaphoreType.DMA
    out = pl.pallas_call(
        functools.partial(kernel, dims),
        out_shape=jax.ShapeDtypeStruct((q, w_all, boxes), BF),
        in_specs=[pl.BlockSpec(memory_space=pltpu.VMEM)] * 12,
        out_specs=pl.BlockSpec(memory_space=pltpu.VMEM),
        scratch_shapes=[
            pltpu.VMEM((n_maps, QP, QP), BF),
            pltpu.VMEM((QP * 16, boxes), F32),
            pltpu.VMEM((w_all, boxes, QP), BF),
            pltpu.VMEM((wc, 8 * par, QP), BF),
            pltpu.VMEM((chunks, wc, par, QP), BF),
            pltpu.VMEM((chunks, wc, par, QP), BF),
            pltpu.VMEM((2, nbox * CAP * wc, 128), F32),
            pltpu.VMEM((chunks, nbox, CAP * wc, QP), BF),
            pltpu.VMEM((chunks, nbox, CAP * wc, QP), BF),
            pltpu.VMEM((wc, pairs, QP), BF),
            pltpu.VMEM((wc, pairs, QP), BF),
            pltpu.VMEM((wc, boxes, QP), F32),
            pltpu.VMEM((chunks, wc, par, QP), BF),
            pltpu.VMEM((chunks, wc, par, QP), BF),
            pltpu.VMEM((wc, 8 * par, QP), BF),
            pltpu.VMEM((q * 16, boxes), F32),
            dma((chunks,)), dma((chunks,)), dma((chunks,)), dma((chunks,)),
            dma((chunks, nbox)), dma((chunks, nbox)), dma((chunks,)),
        ],
        compiler_params=pltpu.CompilerParams(
            collective_id=0, has_side_effects=True, vmem_limit_bytes=60 * 1024 * 1024
        ),
    )(
        sources[0], upward_maps, downward_maps, cross_maps, child_octant, child_parent, parent_box,
        send_index[0, 0], near_source[0], near_target[0], far_source[0], far_target[0],
    )
    return out[None]


def solution(mesh):
    placed = (
        P("leaf", None, None, "box"),
        P(),
        P(),
        P(),
        P("leaf", "box"),
        P("leaf", "box"),
        P("leaf", "box"),
        P("leaf", "box", None, None),
        P("leaf", None, "box"),
        P("leaf", None, "box"),
        P("leaf", None, "box"),
        P("leaf", None, "box"),
    )
    return jax.shard_map(
        per_device,
        mesh=mesh,
        in_specs=placed,
        out_specs=P("leaf", None, None, "box"),
        check_vma=False,
    )
```

time: 753 us -> 205 us (0.27)
  the two profiles are of different devices: /device:TPU:1 before, /device:TPU:31 now
where the time goes in v1:
time: 205 us; the launch traced here: 204 us
  Pallas kernels  199 us (97%)
  local copies, waits for them, and re-layouts  5.95 us (3%)
    pallas_call x1, Pallas kernels, per_device(): pl.pallas_call(functools.partial(kernel, dims), out_shape=jax.ShapeDtypeS...  199 us
    unnamed x1, local copies, waits for them, and re-layouts  4.58 us

profile of v1, /device:TPU:31, one launch (start us, length us, event | category | flops | bytes accessed | tf_op | source)
XLA Modules:
  0.0 204.5 jit_solution(15709752984858609369)
XLA Ops:
  0.0 1.4 copy.13.send_index_ref
  1.4 198.5 %shard_map.118 = bf16[216,64,128]{2,1,0:T(8,128)(2,1)} custom-call(bf16[216,64,128]{2,1,0:T(8,128)(2,1)} %bitcast.8, bf16[8,216,216]{2,1,0:T(8,128)(2,1)} %up_ref.1, bf16[8,216,216]{2,1,0:T(8,128)(2,1)} %down_ref.1, bf16[16,216,216]{2,1,0:T(8,128)(2,1)} %cross_ref.1, s32[1,128]{1,0:T(1,128)} %octant_ref.1, s32[1,128]{1,0:T(1,128)} %parent_ref.1, ...), custom_call_target="tpu_custom_call" | custom-call | tf_op jit(solution)/shard_map/pallas_call | solution.py:336
  199.9 4.6 %copy.15 = bf16[1,216,64,128]{3,2,1,0:T(8,128)(2,1)} copy(bf16[1,216,64,128]{3,2,1,0:T(8,128)(2,1)} %bitcast.7) | data formatting | bytes 7077888

commit v2 on v1

v2 whole, which is shorter than its diff:
```python
import functools

import jax
import jax.numpy as jnp
from jax import lax
from jax.experimental import pallas as pl
from jax.experimental.pallas import tpu as pltpu
from jax.sharding import PartitionSpec as P

BF = jnp.bfloat16
F32 = jnp.float32
MESH = pl.DeviceIdType.MESH
QP = 256
CAP = 4


def dot_nn(a, b):
    return lax.dot_general(a, b, (((1,), (0,)), ((), ())), preferred_element_type=F32)


def dot_nt(a, b):
    return lax.dot_general(a, b, (((1,), (1,)), ((), ())), preferred_element_type=F32)


def iota(shape, dim):
    return lax.broadcasted_iota(jnp.int32, shape, dim)


def onehot(mask):
    return mask.astype(F32).astype(BF)


def column_of(table, by_column):
    a, b = table.shape
    n = a * b
    row = iota((n, 1), 0)
    of_a, of_b = (row % a, row // a) if by_column else (row // b, row % b)
    picked = dot_nn(onehot(of_a == iota((n, a), 1)), table.astype(F32).astype(BF))
    return jnp.sum(jnp.where(of_b == iota((n, b), 1), picked, 0.0), axis=1, keepdims=True)


def is_at(column, width):
    return onehot(column == iota((column.shape[0], width), 1).astype(F32))


def repeat(count, body, unroll=1):
    def step(index, carry):
        body(index)
        return carry

    lax.fori_loop(0, count, step, 0, unroll=unroll)


def kernel(
    dims,
    x_hbm, up_hbm, down_hbm, cross_hbm, octant_ref, parent_ref, slots_ref,
    send_index_ref, near_src_ref, near_dst_ref, far_src_ref, far_dst_ref,
    out_hbm,
    x_in, up_in, down_in, cross_in, up_maps, down_maps, cross_maps,
    x32, m_buf, x_slot, base, bucket, cin, cout, st, send, recv, gath, moved, far, far_slot,
    ein, eout, shift, ost, out_v,
    sem_in, sem_cs, sem_cr, sem_es, sem_er, sem_as, sem_ar, sem_own, sem_out,
):
    nbox, nleaf, q, w_all, boxes, par, wc, ws, rows_k = dims
    chunks, subs = w_all // wc, wc // ws
    rest = q - 128
    me = lax.axis_index("box")
    level = lax.axis_index("leaf")
    last = nleaf - 1

    barrier = pltpu.get_barrier_semaphore()

    @pl.when(level > 0)
    def _():
        pl.semaphore_signal(barrier, inc=1, device_id={"leaf": level - 1}, device_id_type=MESH)

    @pl.when(level < last)
    def _():
        pl.semaphore_signal(barrier, inc=1, device_id={"leaf": level + 1}, device_id_type=MESH)

    @functools.partial(repeat, nbox - 1)
    def _(j):
        pl.semaphore_signal(
            barrier, inc=1, device_id={"box": lax.rem(me + j + 1, nbox)}, device_id_type=MESH
        )

    def x_copy(c):
        return pltpu.make_async_copy(
            x_hbm.at[:, pl.ds(pl.multiple_of(c * wc, 16), wc), :], x_in.at[c], sem_in.at[c]
        )

    def out_copy(c):
        return pltpu.make_async_copy(
            out_v.at[c], out_hbm.at[:, pl.ds(pl.multiple_of(c * wc, 16), wc), :], sem_out.at[c]
        )

    copy_up = pltpu.make_async_copy(up_hbm, up_in, sem_in.at[chunks])
    copy_down = pltpu.make_async_copy(down_hbm, down_in, sem_in.at[chunks + 1])
    copy_cross = pltpu.make_async_copy(cross_hbm, cross_in, sem_in.at[chunks + 2])
    x_copy(0).start()
    copy_up.start()
    for c in range(1, chunks):
        x_copy(c).start()
    copy_down.start()
    copy_cross.start()

    bucket_row = octant_ref[...] * par + parent_ref[...]
    oh_bucket = onehot(bucket_row == iota((8 * par, boxes), 0))
    oh_slot = is_at(column_of(slots_ref[...], False), boxes)
    oh_slot_t = onehot(slots_ref[...] == iota((boxes, par), 0))
    in_slots = jnp.max(oh_slot.astype(F32), axis=0, keepdims=True)
    oh_bucket_base = (oh_bucket.astype(F32) * (1.0 - in_slots)).astype(BF)
    oh_bucket_slot = dot_nn(oh_bucket, oh_slot_t).astype(BF)
    oh_send = is_at(column_of(send_index_ref[...], False), boxes)

    def turn_maps(source, target, count):
        @functools.partial(repeat, count, unroll=2)
        def _(k):
            target[k] = jnp.zeros((QP, QP), BF)
            target[k, 0:q, 0:q] = source[k].astype(F32).T.astype(BF)

    @pl.when(level == last)
    def _():
        cin[...] = jnp.zeros_like(cin)

    @pl.when(level == 0)
    def _():
        ein[...] = jnp.zeros_like(ein)

    def chain(buf_from, buf_to, c, s_sem, r_sem, target):
        return pltpu.make_async_remote_copy(
            src_ref=buf_from.at[c], dst_ref=buf_to.at[c], send_sem=s_sem.at[c], recv_sem=r_sem.at[c],
            device_id={"leaf": target}, device_id_type=MESH,
        )

    def upward(c):
        return chain(cout, cin, c, sem_cs, sem_cr, jnp.maximum(level - 1, 0))

    def downward(c):
        return chain(eout, ein, c, sem_es, sem_er, jnp.minimum(level + 1, last))

    def exchange(c, j):
        to = lax.rem(me + j, nbox)
        return pltpu.make_async_remote_copy(
            src_ref=send.at[c, to], dst_ref=recv.at[c, me], send_sem=sem_as.at[c, j],
            recv_sem=sem_ar.at[c, j], device_id={"box": to}, device_id_type=MESH,
        )

    def from_peer(c, j):
        peer = lax.rem(me + nbox - j, nbox)
        return pltpu.make_async_remote_copy(
            src_ref=send.at[c, peer], dst_ref=recv.at[c, peer], send_sem=sem_as.at[c, j],
            recv_sem=sem_ar.at[c, j], device_id={"box": peer}, device_id_type=MESH,
        )

    def own_copy(c):
        return pltpu.make_async_copy(send.at[c, me], recv.at[c, me], sem_own.at[c])

    x32[q * wc :, :] = jnp.zeros(((QP - q) * wc, boxes), F32)

    def prepare(c):
        x_copy(c).wait()
        x32[0 : q * wc, :] = x_in[c].astype(F32).reshape(q * wc, boxes)

        @functools.partial(repeat, wc, unroll=8)
        def _(w):
            x_w = x32[pl.ds(w, QP, stride=wc), :].T.astype(BF)
            m_buf[c * wc + w] = x_w
            x_slot[w] = dot_nn(oh_slot, x_w)
            base[w] = dot_nn(oh_bucket_base, x_w)

    def climb(c, s):
        @pl.when(level < last)
        def _():
            upward(c * subs + s).wait_recv()

        for w in range(ws):
            at = s * ws + w
            slot_w = (x_slot[at] + cin[c * subs + s, w].astype(F32)).astype(BF)
            bucket[w] = (base[at] + dot_nn(oh_bucket_slot, slot_w)).astype(BF)
        rows = jnp.concatenate(
            [bucket[:, o * par : (o + 1) * par, :].reshape(ws * par, QP) for o in range(8)], axis=1
        )
        total = dot_nn(rows, up_maps[...].reshape(8 * QP, QP))
        cout[c * subs + s] = total.astype(BF).reshape(ws, par, QP)

        @pl.when(level > 0)
        def _():
            upward(c * subs + s).start()

    lane = iota((nbox, 128), 1)

    def hand_out(c):
        @functools.partial(repeat, wc, unroll=8)
        def _(w):
            at = c * wc + w
            c_w = cin[c * subs + w // ws, w % ws]
            m_w = (m_buf[at].astype(F32) + dot_nn(oh_slot_t, c_w)).astype(BF)
            m_buf[at] = m_w
            o_w = dot_nn(oh_send, m_w)
            tails = []
            for i in range(CAP):
                part = o_w[i * nbox : (i + 1) * nbox]
                st[i, pl.ds(w, nbox, stride=wc), :] = part[:, 0:128]
                tail = part[:, 128:QP]
                tails.append(pltpu.roll(tail, (i * rest) % 128, 1) if i else tail)
            for t in range(CAP - 1):
                packed = jnp.where(lane < (t + 1) * rest - t * 128, tails[t], tails[t + 1])
                st[CAP + t, pl.ds(w, nbox, stride=wc), :] = packed

        for t in range(2 * CAP - 1):
            send[c, :, t * wc : (t + 1) * wc, :] = st[t].astype(BF).reshape(nbox, wc, 128)

        @functools.partial(repeat, nbox - 1)
        def _(j):
            exchange(c, j + 1).start()

        own_copy(c).start()

    copy_up.wait()
    turn_maps(up_in, up_maps, 8)
    prepare(0)
    pl.semaphore_wait(
        barrier, nbox + 1 - (level == 0).astype(jnp.int32) - (level == last).astype(jnp.int32)
    )

    @functools.partial(repeat, chunks)
    def _(c):
        @pl.when(c > 0)
        def _():
            prepare(c)

        for s in range(subs):
            climb(c, s)
        hand_out(c)

    oh_near_src = is_at(column_of(near_src_ref[...], False), boxes)
    far_src = far_src_ref[...]
    oh_far_src = is_at(column_of((far_src % CAP) * nbox + far_src // CAP, False), CAP * nbox)
    near_dst = is_at(column_of(near_dst_ref[...], False), boxes).astype(F32)
    far_dst = is_at(column_of(far_dst_ref[...], False), boxes).astype(F32)
    oh_near_dst = near_dst.T.astype(BF)
    oh_far_dst = far_dst.T.astype(BF)
    oh_near_slot = dot_nn(oh_slot, oh_near_dst).astype(BF)
    oh_far_slot = dot_nn(oh_slot, oh_far_dst).astype(BF)
    oh_bucket_t = oh_bucket.astype(F32).T.astype(BF)
    oh_slot_bucket = dot_nn(oh_slot, oh_bucket_t).astype(BF)
    copy_down.wait()
    turn_maps(down_in, down_maps, 8)
    copy_cross.wait()
    turn_maps(cross_in, cross_maps, cross_in.shape[0])

    def apply_cross():
        @functools.partial(repeat, cross_in.shape[0], unroll=4)
        def _(k):
            at = pl.ds(pl.multiple_of(k * rows_k, 16), rows_k)
            moved[:, at, :] = (
                dot_nn(gath[:, at, :].reshape(wc * rows_k, QP), cross_maps[k])
                .astype(BF)
                .reshape(wc, rows_k, QP)
            )

    def near_field(c):
        @functools.partial(repeat, wc, unroll=8)
        def _(w):
            gath[w] = dot_nn(oh_near_src, m_buf[c * wc + w]).astype(BF)

        apply_cross()

        @functools.partial(repeat, wc, unroll=8)
        def _(w):
            far[w] = dot_nn(oh_near_dst, moved[w])
            far_slot[w] = dot_nn(oh_near_slot, moved[w])

    def far_field(c):
        for t in range(2 * CAP - 1):
            st[t] = recv[c, :, t * wc : (t + 1) * wc, :].astype(F32).reshape(nbox * wc, 128)

        @functools.partial(repeat, wc, unroll=4)
        def _(w):
            tiles = [st[t, pl.ds(w, nbox, stride=wc), :] for t in range(2 * CAP - 1)]
            parts = []
            for i in range(CAP):
                if i == 0:
                    tail = tiles[CAP]
                else:
                    tail = tiles[CAP + i - 1]
                    if i < CAP - 1:
                        tail = jnp.where(lane >= i * rest - (i - 1) * 128, tail, tiles[CAP + i])
                    tail = pltpu.roll(tail, (-i * rest) % 128, 1)
                tail = jnp.where(lane < rest, tail, 0.0)
                parts.append(jnp.concatenate([tiles[i], tail], axis=1))
            gath[w] = dot_nn(oh_far_src, jnp.concatenate(parts, axis=0).astype(BF)).astype(BF)

        apply_cross()

        @functools.partial(repeat, wc, unroll=8)
        def _(w):
            far[w] += dot_nn(oh_far_dst, moved[w])
            far_slot[w] += dot_nn(oh_far_slot, moved[w])

    def descend(c, s):
        @pl.when(level > 0)
        def _():
            downward(c * subs + s).wait_recv()

        rows = ein[c * subs + s].reshape(ws * par, QP)
        for o in range(8):
            shift[s * ws : (s + 1) * ws, o * par : (o + 1) * par, :] = (
                dot_nn(rows, down_maps[o]).astype(BF).reshape(ws, par, QP)
            )
        for w in range(ws):
            at = s * ws + w
            eout[c * subs + s, w] = (far_slot[at] + dot_nn(oh_slot_bucket, shift[at])).astype(BF)

        @pl.when(level < last)
        def _():
            downward(c * subs + s).start()

    def deliver(c):
        @functools.partial(repeat, wc, unroll=4)
        def _(w):
            e_w = far[w] + dot_nn(oh_bucket_t, shift[w])
            ost[pl.ds(w, q, stride=wc), :] = e_w.T[0:q, :]

        out_v[c] = ost[...].reshape(q, wc, boxes).astype(BF)
        out_copy(c).start()

    @functools.partial(repeat, chunks)
    def _(c):
        near_field(c)

        @functools.partial(repeat, nbox - 1)
        def _(j):
            from_peer(c, j + 1).wait_recv()

        own_copy(c).wait()
        far_field(c)
        for s in range(subs):
            descend(c, s)
        deliver(c)

    @functools.partial(repeat, chunks)
    def _(c):
        @functools.partial(repeat, nbox - 1)
        def _(j):
            exchange(c, j + 1).wait_send()

        for s in range(subs):
            @pl.when(level > 0)
            def _():
                upward(c * subs + s).wait_send()

            @pl.when(level < last)
            def _():
                downward(c * subs + s).wait_send()

        out_copy(c).wait()


def copy_kernel(a_ref, b_ref):
    b_ref[...] = a_ref[...]


def per_device(
    sources, upward_maps, downward_maps, cross_maps, child_octant, child_parent, parent_box,
    send_index, near_source, near_target, far_source, far_target,
):
    nbox, nleaf = lax.axis_size("box"), lax.axis_size("leaf")
    _, q, w_all, boxes = sources.shape
    par = parent_box.shape[1]
    rows_k = near_source.shape[2]
    pairs = near_source.shape[1] * rows_k
    wc, ws = 16, 8
    chunks, n_sub = w_all // wc, w_all // ws
    dims = (nbox, nleaf, q, w_all, boxes, par, wc, ws, rows_k)
    dma = pltpu.SemaphoreType.DMA
    any_spec = pl.BlockSpec(memory_space=pl.ANY)
    vmem_spec = pl.BlockSpec(memory_space=pltpu.VMEM)
    n_cross = cross_maps.shape[0]
    out = pl.pallas_call(
        functools.partial(kernel, dims),
        out_shape=jax.ShapeDtypeStruct((q, w_all, boxes), BF),
        in_specs=[any_spec] * 4 + [vmem_spec] * 8,
        out_specs=any_spec,
        scratch_shapes=[
            pltpu.VMEM((chunks, q, wc, boxes), BF),
            pltpu.VMEM(upward_maps.shape, BF),
            pltpu.VMEM(downward_maps.shape, BF),
            pltpu.VMEM(cross_maps.shape, BF),
            pltpu.VMEM((8, QP, QP), BF),
            pltpu.VMEM((8, QP, QP), BF),
            pltpu.VMEM((n_cross, QP, QP), BF),
            pltpu.VMEM((QP * wc, boxes), F32),
            pltpu.VMEM((w_all, boxes, QP), BF),
            pltpu.VMEM((wc, par, QP), F32),
            pltpu.VMEM((wc, 8 * par, QP), F32),
            pltpu.VMEM((ws, 8 * par, QP), BF),
            pltpu.VMEM((n_sub, ws, par, QP), BF),
            pltpu.VMEM((n_sub, ws, par, QP), BF),
            pltpu.VMEM((2 * CAP - 1, nbox * wc, 128), F32),
            pltpu.VMEM((chunks, nbox, (2 * CAP - 1) * wc, 128), BF),
            pltpu.VMEM((chunks, nbox, (2 * CAP - 1) * wc, 128), BF),
            pltpu.VMEM((wc, pairs, QP), BF),
            pltpu.VMEM((wc, pairs, QP), BF),
            pltpu.VMEM((wc, boxes, QP), F32),
            pltpu.VMEM((wc, par, QP), F32),
            pltpu.VMEM((n_sub, ws, par, QP), BF),
            pltpu.VMEM((n_sub, ws, par, QP), BF),
            pltpu.VMEM((wc, 8 * par, QP), BF),
            pltpu.VMEM((q * wc, boxes), F32),
            pltpu.VMEM((chunks, q, wc, boxes), BF),
            dma((chunks + 3,)),
            dma((n_sub,)), dma((n_sub,)), dma((n_sub,)), dma((n_sub,)),
            dma((chunks, nbox)), dma((chunks, nbox)), dma((chunks,)), dma((chunks,)),
        ],
        compiler_params=pltpu.CompilerParams(
            collective_id=0, has_side_effects=True, vmem_limit_bytes=60 * 1024 * 1024
        ),
    )(
        sources[0], upward_maps, downward_maps, cross_maps, child_octant, child_parent, parent_box,
        send_index[0, 0].T, near_source[0], near_target[0], far_source[0], far_target[0],
    )
    block = pl.BlockSpec((q // 9, w_all, boxes), lambda i: (i, 0, 0))
    out = pl.pallas_call(
        copy_kernel,
        grid=(9,),
        out_shape=jax.ShapeDtypeStruct((q, w_all, boxes), BF),
        in_specs=[block],
        out_specs=block,
        compiler_params=pltpu.CompilerParams(vmem_limit_bytes=8 * 1024 * 1024),
    )(out)
    return out[None]


def solution(mesh):
    placed = (
        P("leaf", None, None, "box"),
        P(),
        P(),
        P(),
        P("leaf", "box"),
        P("leaf", "box"),
        P("leaf", "box"),
        P("leaf", "box", None, None),
        P("leaf", None, "box"),
        P("leaf", None, "box"),
        P("leaf", None, "box"),
        P("leaf", None, "box"),
    )
    return jax.shard_map(
        per_device,
        mesh=mesh,
        in_specs=placed,
        out_specs=P("leaf", None, None, "box"),
        check_vma=False,
    )
```

time: 205 us -> 143 us (0.70)
  Pallas kernels: 199 us -> 140 us
  local copies, waits for them, and re-layouts: 5.95 us -> 1.99 us
    pallas_call x1, Pallas kernels: 199 us -> 137 us  [per_device(): pl.pallas_call(functools.partial(kernel, dims), out_shape=jax.ShapeDtypeS...]
    pallas_call x0 -> x1, Pallas kernels: none -> 3.85 us  [per_device(): pl.pallas_call(copy_kernel, grid=(9,), out_shape=jax.ShapeDtypeStruct((q,...]
    unnamed x1 -> x2, local copies, waits for them, and re-layouts: 4.58 us -> 1.99 us
where the time goes in v2:
time: 143 us; the launch traced here: 142 us
  Pallas kernels  140 us (98%)
  local copies, waits for them, and re-layouts  1.99 us (1%)
    pallas_call x1, Pallas kernels, per_device(): pl.pallas_call(functools.partial(kernel, dims), out_shape=jax.ShapeDtypeS...  137 us
    pallas_call x1, Pallas kernels, per_device(): pl.pallas_call(copy_kernel, grid=(9,), out_shape=jax.ShapeDtypeStruct((q,...  3.85 us

profile of v2, /device:TPU:31, one launch (start us, length us, event | category | flops | bytes accessed | tf_op | source)
XLA Modules:
  0.0 142.4 jit_solution(11987799577240834829)
XLA Ops:
  0.0 136.5 %shard_map.118.a_ref = bf16[216,64,128]{2,1,0:T(8,128)(2,1)} custom-call(bf16[216,64,128]{2,1,0:T(8,128)(2,1)} %bitcast.9, bf16[8,216,216]{2,1,0:T(8,128)(2,1)} %up_hbm.1, bf16[8,216,216]{2,1,0:T(8,128)(2,1)} %down_hbm.1, bf16[16,216,216]{2,1,0:T(8,128)(2,1)} %cross_hbm.1, s32[1,128]{1,0:T(1,128)} %octant_ref.1, s32[1,128]{1,0:T(1,128)} %parent_ref.1, ...), custom_call_target="tpu_custom_call" | custom-call | tf_op jit(solution)/shard_map/pallas_call | solution.py:381
  136.5 0.0 copy-start
  136.5 2.0 %copy-done = bf16[216,64,128]{2,1,0:T(8,128)(2,1)S(1)} copy-done((bf16[216,64,128]{2,1,0:T(8,128)(2,1)S(1)}, bf16[216,64,128]{2,1,0:T(8,128)(2,1)}, u32[]{:S(2)}) %copy-start) | copy-done | bytes 3538968
  138.5 3.9 %shard_map.119 = bf16[216,64,128]{2,1,0:T(8,128)(2,1)} custom-call(bf16[216,64,128]{2,1,0:T(8,128)(2,1)S(1)} %copy-done), custom_call_target="tpu_custom_call" | custom-call | tf_op jit(solution)/shard_map/pallas_call | solution.py:425
Async XLA Ops:
  136.5 2.0 %copy-start = (bf16[216,64,128]{2,1,0:T(8,128)(2,1)S(1)}, bf16[216,64,128]{2,1,0:T(8,128)(2,1)}, u32[]{:S(2)}) copy-start(bf16[216,64,128]{2,1,0:T(8,128)(2,1)} %shard_map.118.a_ref) | copy-start | bytes 10616836

commit v3 on v2

--- a/solution.py
+++ b/solution.py
@@ -53,13 +53,15 @@
 
 def kernel(
     dims,
-    x_hbm, up_hbm, down_hbm, cross_hbm, octant_ref, parent_ref, slots_ref,
+    x_hbm, up_hbm, down_hbm, cross_hbm, octant_hbm, parent_hbm, slots_hbm,
+    send_index_hbm, near_src_hbm, near_dst_hbm, far_src_hbm, far_dst_hbm,
+    out_hbm,
+    octant_ref, parent_ref, slots_ref,
     send_index_ref, near_src_ref, near_dst_ref, far_src_ref, far_dst_ref,
-    out_hbm,
     x_in, up_in, down_in, cross_in, up_maps, down_maps, cross_maps,
     x32, m_buf, x_slot, base, bucket, cin, cout, st, send, recv, gath, moved, far, far_slot,
     ein, eout, shift, ost, out_v,
-    sem_in, sem_cs, sem_cr, sem_es, sem_er, sem_as, sem_ar, sem_own, sem_out,
+    sem_int, sem_in, sem_cs, sem_cr, sem_es, sem_er, sem_as, sem_ar, sem_own, sem_out,
 ):
     nbox, nleaf, q, w_all, boxes, par, wc, ws, rows_k = dims
     chunks, subs = w_all // wc, wc // ws
@@ -70,6 +72,34 @@
 
     barrier = pltpu.get_barrier_semaphore()
 
+    def x_copy(c):
+        return pltpu.make_async_copy(
+            x_hbm.at[:, pl.ds(pl.multiple_of(c * wc, 16), wc), :], x_in.at[c], sem_in.at[c]
+        )
+
+    def out_copy(c):
+        return pltpu.make_async_copy(
+            out_v.at[c], out_hbm.at[:, pl.ds(pl.multiple_of(c * wc, 16), wc), :], sem_out.at[c]
+        )
+
+    copy_up = pltpu.make_async_copy(up_hbm, up_in, sem_in.at[chunks])
+    copy_down = pltpu.make_async_copy(down_hbm, down_in, sem_in.at[chunks + 1])
+    copy_cross = pltpu.make_async_copy(cross_hbm, cross_in, sem_in.at[chunks + 2])
+    int_copies = [
+        pltpu.make_async_copy(source, target, sem_int.at[i])
+        for i, (source, target) in enumerate(
+            (
+                (octant_hbm, octant_ref), (parent_hbm, parent_ref), (slots_hbm, slots_ref),
+                (send_index_hbm, send_index_ref), (near_src_hbm, near_src_ref),
+                (near_dst_hbm, near_dst_ref), (far_src_hbm, far_src_ref), (far_dst_hbm, far_dst_ref),
+            )
+        )
+    ]
+    for one in int_copies:
+        one.start()
+    x_copy(0).start()
+    copy_up.start()
+
     @pl.when(level > 0)
     def _():
         pl.semaphore_signal(barrier, inc=1, device_id={"leaf": level - 1}, device_id_type=MESH)
@@ -84,25 +114,12 @@
             barrier, inc=1, device_id={"box": lax.rem(me + j + 1, nbox)}, device_id_type=MESH
         )
 
-    def x_copy(c):
-        return pltpu.make_async_copy(
-            x_hbm.at[:, pl.ds(pl.multiple_of(c * wc, 16), wc), :], x_in.at[c], sem_in.at[c]
-        )
-
-    def out_copy(c):
-        return pltpu.make_async_copy(
-            out_v.at[c], out_hbm.at[:, pl.ds(pl.multiple_of(c * wc, 16), wc), :], sem_out.at[c]
-        )
-
-    copy_up = pltpu.make_async_copy(up_hbm, up_in, sem_in.at[chunks])
-    copy_down = pltpu.make_async_copy(down_hbm, down_in, sem_in.at[chunks + 1])
-    copy_cross = pltpu.make_async_copy(cross_hbm, cross_in, sem_in.at[chunks + 2])
-    x_copy(0).start()
-    copy_up.start()
     for c in range(1, chunks):
         x_copy(c).start()
     copy_down.start()
     copy_cross.start()
+    for one in int_copies:
+        one.wait()
 
     bucket_row = octant_ref[...] * par + parent_ref[...]
     oh_bucket = onehot(bucket_row == iota((8 * par, boxes), 0))
@@ -276,7 +293,7 @@
         for t in range(2 * CAP - 1):
             st[t] = recv[c, :, t * wc : (t + 1) * wc, :].astype(F32).reshape(nbox * wc, 128)
 
-        @functools.partial(repeat, wc, unroll=4)
+        @functools.partial(repeat, wc, unroll=8)
         def _(w):
             tiles = [st[t, pl.ds(w, nbox, stride=wc), :] for t in range(2 * CAP - 1)]
             parts = []
@@ -318,7 +335,7 @@
             downward(c * subs + s).start()
 
     def deliver(c):
-        @functools.partial(repeat, wc, unroll=4)
+        @functools.partial(repeat, wc, unroll=8)
         def _(w):
             e_w = far[w] + dot_nn(oh_bucket_t, shift[w])
             ost[pl.ds(w, q, stride=wc), :] = e_w.T[0:q, :]
@@ -358,8 +375,18 @@
         out_copy(c).wait()
 
 
-def copy_kernel(a_ref, b_ref):
-    b_ref[...] = a_ref[...]
+def copy_kernel(parts, a_ref, b_ref, held, sems):
+    size = a_ref.shape[0] // parts
+    at = [pl.ds(i * size, size) for i in range(parts)]
+    inward = [pltpu.make_async_copy(a_ref.at[at[i]], held.at[at[i]], sems.at[0, i]) for i in range(parts)]
+    outward = [pltpu.make_async_copy(held.at[at[i]], b_ref.at[at[i]], sems.at[1, i]) for i in range(parts)]
+    for one in inward:
+        one.start()
+    for i in range(parts):
+        inward[i].wait()
+        outward[i].start()
+    for one in outward:
+        one.wait()
 
 
 def per_device(
@@ -371,19 +398,23 @@
     par = parent_box.shape[1]
     rows_k = near_source.shape[2]
     pairs = near_source.shape[1] * rows_k
-    wc, ws = 16, 8
+    wc, ws = 16, 4
     chunks, n_sub = w_all // wc, w_all // ws
     dims = (nbox, nleaf, q, w_all, boxes, par, wc, ws, rows_k)
+    integers = (
+        child_octant, child_parent, parent_box, send_index[0, 0].T,
+        near_source[0], near_target[0], far_source[0], far_target[0],
+    )
     dma = pltpu.SemaphoreType.DMA
     any_spec = pl.BlockSpec(memory_space=pl.ANY)
-    vmem_spec = pl.BlockSpec(memory_space=pltpu.VMEM)
     n_cross = cross_maps.shape[0]
     out = pl.pallas_call(
         functools.partial(kernel, dims),
         out_shape=jax.ShapeDtypeStruct((q, w_all, boxes), BF),
-        in_specs=[any_spec] * 4 + [vmem_spec] * 8,
+        in_specs=[any_spec] * 12,
         out_specs=any_spec,
-        scratch_shapes=[
+        scratch_shapes=[pltpu.VMEM(one.shape, jnp.int32) for one in integers]
+        + [
             pltpu.VMEM((chunks, q, wc, boxes), BF),
             pltpu.VMEM(upward_maps.shape, BF),
             pltpu.VMEM(downward_maps.shape, BF),
@@ -410,7 +441,7 @@
             pltpu.VMEM((wc, 8 * par, QP), BF),
             pltpu.VMEM((q * wc, boxes), F32),
             pltpu.VMEM((chunks, q, wc, boxes), BF),
-            dma((chunks + 3,)),
+            dma((len(integers),)), dma((chunks + 3,)),
             dma((n_sub,)), dma((n_sub,)), dma((n_sub,)), dma((n_sub,)),
             dma((chunks, nbox)), dma((chunks, nbox)), dma((chunks,)), dma((chunks,)),
         ],
@@ -418,17 +449,16 @@
             collective_id=0, has_side_effects=True, vmem_limit_bytes=60 * 1024 * 1024
         ),
     )(
-        sources[0], upward_maps, downward_maps, cross_maps, child_octant, child_parent, parent_box,
-        send_index[0, 0].T, near_source[0], near_target[0], far_source[0], far_target[0],
+        sources[0], upward_maps, downward_maps, cross_maps, *integers
     )
-    block = pl.BlockSpec((q // 9, w_all, boxes), lambda i: (i, 0, 0))
+    parts = 8
     out = pl.pallas_call(
-        copy_kernel,
-        grid=(9,),
+        functools.partial(copy_kernel, parts),
         out_shape=jax.ShapeDtypeStruct((q, w_all, boxes), BF),
-        in_specs=[block],
-        out_specs=block,
-        compiler_params=pltpu.CompilerParams(vmem_limit_bytes=8 * 1024 * 1024),
+        in_specs=[any_spec],
+        out_specs=any_spec,
+        scratch_shapes=[pltpu.VMEM((q, w_all, boxes), BF), dma((2, parts))],
+        compiler_params=pltpu.CompilerParams(vmem_limit_bytes=60 * 1024 * 1024),
     )(out)
     return out[None]
 

time: 143 us -> 137 us (0.958)
  Pallas kernels: 140 us -> 136 us
  local copies, waits for them, and re-layouts: 1.99 us -> 0 us
    pallas_call x1, Pallas kernels: 137 us -> 133 us  [per_device(): pl.pallas_call(functools.partial(kernel, dims), out_shape=jax.ShapeDtypeS...]
    unnamed x2 -> x0, local copies, waits for them, and re-layouts: 1.99 us -> none
where the time goes in v3:
time: 137 us; the launch traced here: 136 us
  Pallas kernels  136 us (99%)
    pallas_call x1, Pallas kernels, per_device(): pl.pallas_call(functools.partial(kernel, dims), out_shape=jax.ShapeDtypeS...  133 us
    pallas_call x1, Pallas kernels, per_device(): pl.pallas_call(functools.partial(copy_kernel, parts), out_shape=jax.Shape...  2.93 us

profile of v3, /device:TPU:31, one launch (start us, length us, event | category | flops | bytes accessed | tf_op | source)
XLA Modules:
  0.0 136.4 jit_solution(3889186150386468570)
XLA Ops:
  0.0 133.5 %shard_map.118.a_ref = bf16[216,64,128]{2,1,0:T(8,128)(2,1)} custom-call(bf16[216,64,128]{2,1,0:T(8,128)(2,1)} %bitcast.9, bf16[8,216,216]{2,1,0:T(8,128)(2,1)} %up_hbm.1, bf16[8,216,216]{2,1,0:T(8,128)(2,1)} %down_hbm.1, bf16[16,216,216]{2,1,0:T(8,128)(2,1)} %cross_hbm.1, s32[1,128]{1,0:T(1,128)} %octant_hbm.1, s32[1,128]{1,0:T(1,128)} %parent_hbm.1, ...), custom_call_target="tpu_custom_call" | custom-call | tf_op jit(solution)/shard_map/pallas_call | solution.py:411
  133.5 2.9 %shard_map.119 = bf16[216,64,128]{2,1,0:T(8,128)(2,1)} custom-call(bf16[216,64,128]{2,1,0:T(8,128)(2,1)} %shard_map.118.a_ref), custom_call_target="tpu_custom_call" | custom-call | tf_op jit(solution)/shard_map/pallas_call | solution.py:455

commit v4 on v3

--- a/solution.py
+++ b/solution.py
@@ -12,6 +12,7 @@
 MESH = pl.DeviceIdType.MESH
 QP = 256
 CAP = 4
+RELAYS = (2, 0)
 
 
 def dot_nn(a, b):
@@ -60,8 +61,8 @@
     send_index_ref, near_src_ref, near_dst_ref, far_src_ref, far_dst_ref,
     x_in, up_in, down_in, cross_in, up_maps, down_maps, cross_maps,
     x32, m_buf, x_slot, base, bucket, cin, cout, st, send, recv, gath, moved, far, far_slot,
-    ein, eout, shift, ost, out_v,
-    sem_int, sem_in, sem_cs, sem_cr, sem_es, sem_er, sem_as, sem_ar, sem_own, sem_out,
+    ein, eout, shift, ost, out_v, relay,
+    sem_int, sem_in, sem_cs, sem_cr, sem_es, sem_er, sem_as, sem_ar, sem_own, sem_out, sem_rs, sem_rr,
 ):
     nbox, nleaf, q, w_all, boxes, par, wc, ws, rows_k = dims
     chunks, subs = w_all // wc, wc // ws
@@ -69,8 +70,18 @@
     me = lax.axis_index("box")
     level = lax.axis_index("leaf")
     last = nleaf - 1
+    mirror = nleaf - 2 - level // 2 * 2 + level % 2
+    relayed = [nbox // 2, nbox // 2 + 1, nbox // 2 - 1][: RELAYS[0]]
+    hands_over = [level < 2 * sum(n > r for n in RELAYS) for r in range(len(relayed))]
+    carries = [level >= nleaf - 2 * sum(n > r for n in RELAYS) for r in range(len(relayed))]
 
     barrier = pltpu.get_barrier_semaphore()
+
+    def greet_mirror(offset):
+        pl.semaphore_signal(
+            barrier, inc=1, device_id={"box": lax.rem(me + nbox + offset, nbox), "leaf": mirror},
+            device_id_type=MESH,
+        )
 
     def x_copy(c):
         return pltpu.make_async_copy(
@@ -114,6 +125,22 @@
             barrier, inc=1, device_id={"box": lax.rem(me + j + 1, nbox)}, device_id_type=MESH
         )
 
+    expected = nbox + 1 - (level == 0).astype(jnp.int32) - (level == last).astype(jnp.int32)
+    for r, offset in enumerate(relayed):
+        expected += (hands_over[r] | carries[r]).astype(jnp.int32) * (2 if r == 0 else 1)
+
+        @pl.when(hands_over[r])
+        def _():
+            greet_mirror(-offset)
+            if r == 0:
+                greet_mirror(0)
+
+        @pl.when(carries[r])
+        def _():
+            greet_mirror(offset)
+            if r == 0:
+                greet_mirror(0)
+
     for c in range(1, chunks):
         x_copy(c).start()
     copy_down.start()
@@ -170,6 +197,27 @@
             recv_sem=sem_ar.at[c, j], device_id={"box": peer}, device_id_type=MESH,
         )
 
+    def hand_over(c, r):
+        to = lax.rem(me + relayed[r], nbox)
+        return pltpu.make_async_remote_copy(
+            src_ref=send.at[c, to], dst_ref=relay.at[c, r], send_sem=sem_as.at[c, relayed[r]],
+            recv_sem=sem_rr.at[c, r], device_id={"leaf": mirror}, device_id_type=MESH,
+        )
+
+    def carry_on(c, r):
+        to = lax.rem(me + relayed[r], nbox)
+        return pltpu.make_async_remote_copy(
+            src_ref=relay.at[c, r], dst_ref=recv.at[c, me], send_sem=sem_rs.at[c, r],
+            recv_sem=sem_ar.at[c, relayed[r]], device_id={"box": to, "leaf": mirror}, device_id_type=MESH,
+        )
+
+    def forward(c):
+        for r in range(len(relayed)):
+            @pl.when(carries[r])
+            def _():
+                hand_over(c, r).wait_recv()
+                carry_on(c, r).start()
+
     def own_copy(c):
         return pltpu.make_async_copy(send.at[c, me], recv.at[c, me], sem_own.at[c])
 
@@ -206,6 +254,17 @@
             upward(c * subs + s).start()
 
     lane = iota((nbox, 128), 1)
+
+    def send_direct(c):
+        @functools.partial(repeat, nbox - 1)
+        def _(j):
+            direct = j >= 0
+            for r, offset in enumerate(relayed):
+                direct &= jnp.logical_not(hands_over[r] & (j + 1 == offset))
+
+            @pl.when(direct)
+            def _():
+                exchange(c, j + 1).start()
 
     def hand_out(c):
         @functools.partial(repeat, wc, unroll=8)
@@ -228,18 +287,21 @@
         for t in range(2 * CAP - 1):
             send[c, :, t * wc : (t + 1) * wc, :] = st[t].astype(BF).reshape(nbox, wc, 128)
 
-        @functools.partial(repeat, nbox - 1)
-        def _(j):
-            exchange(c, j + 1).start()
+        for r in range(len(relayed)):
+            @pl.when(hands_over[r])
+            def _():
+                hand_over(c, r).start()
+
+        @pl.when(jnp.logical_not(carries[0]) | (c == 0))
+        def _():
+            send_direct(c)
 
         own_copy(c).start()
 
     copy_up.wait()
     turn_maps(up_in, up_maps, 8)
     prepare(0)
-    pl.semaphore_wait(
-        barrier, nbox + 1 - (level == 0).astype(jnp.int32) - (level == last).astype(jnp.int32)
-    )
+    pl.semaphore_wait(barrier, expected)
 
     @functools.partial(repeat, chunks)
     def _(c):
@@ -347,12 +409,20 @@
     def _(c):
         near_field(c)
 
+        @pl.when(carries[0] & (c == 0))
+        def _():
+            forward(0)
+            for one in range(1, chunks):
+                forward(one)
+                send_direct(one)
+
         @functools.partial(repeat, nbox - 1)
         def _(j):
             from_peer(c, j + 1).wait_recv()
 
         own_copy(c).wait()
         far_field(c)
+
         for s in range(subs):
             descend(c, s)
         deliver(c)
@@ -371,6 +441,11 @@
             @pl.when(level < last)
             def _():
                 downward(c * subs + s).wait_send()
+
+        for r in range(len(relayed)):
+            @pl.when(carries[r])
+            def _():
+                carry_on(c, r).wait_send()
 
         out_copy(c).wait()
 
@@ -441,9 +516,11 @@
             pltpu.VMEM((wc, 8 * par, QP), BF),
             pltpu.VMEM((q * wc, boxes), F32),
             pltpu.VMEM((chunks, q, wc, boxes), BF),
+            pltpu.VMEM((chunks, RELAYS[0], (2 * CAP - 1) * wc, 128), BF),
             dma((len(integers),)), dma((chunks + 3,)),
             dma((n_sub,)), dma((n_sub,)), dma((n_sub,)), dma((n_sub,)),
             dma((chunks, nbox)), dma((chunks, nbox)), dma((chunks,)), dma((chunks,)),
+            dma((chunks, RELAYS[0])), dma((chunks, RELAYS[0])),
         ],
         compiler_params=pltpu.CompilerParams(
             collective_id=0, has_side_effects=True, vmem_limit_bytes=60 * 1024 * 1024

time: 137 us -> 131 us (0.956)
  Pallas kernels: 136 us -> 130 us
    pallas_call x1, Pallas kernels: 133 us -> 127 us  [per_device(): pl.pallas_call(functools.partial(kernel, dims), out_shape=jax.ShapeDtypeS...]
where the time goes in v4:
time: 131 us; the launch traced here: 130 us
  Pallas kernels  130 us (99%)
    pallas_call x1, Pallas kernels, per_device(): pl.pallas_call(functools.partial(kernel, dims), out_shape=jax.ShapeDtypeS...  127 us
    pallas_call x1, Pallas kernels, per_device(): pl.pallas_call(functools.partial(copy_kernel, parts), out_shape=jax.Shape...  2.93 us

profile of v4, /device:TPU:31, one launch (start us, length us, event | category | flops | bytes accessed | tf_op | source)
XLA Modules:
  0.0 130.1 jit_solution(12678659484387429305)
XLA Ops:
  0.0 127.2 %shard_map.118.a_ref = bf16[216,64,128]{2,1,0:T(8,128)(2,1)} custom-call(bf16[216,64,128]{2,1,0:T(8,128)(2,1)} %bitcast.9, bf16[8,216,216]{2,1,0:T(8,128)(2,1)} %up_hbm.1, bf16[8,216,216]{2,1,0:T(8,128)(2,1)} %down_hbm.1, bf16[16,216,216]{2,1,0:T(8,128)(2,1)} %cross_hbm.1, s32[1,128]{1,0:T(1,128)} %octant_hbm.1, s32[1,128]{1,0:T(1,128)} %parent_hbm.1, ...), custom_call_target="tpu_custom_call" | custom-call | tf_op jit(solution)/shard_map/pallas_call | solution.py:486
  127.2 2.9 %shard_map.119 = bf16[216,64,128]{2,1,0:T(8,128)(2,1)} custom-call(bf16[216,64,128]{2,1,0:T(8,128)(2,1)} %shard_map.118.a_ref), custom_call_target="tpu_custom_call" | custom-call | tf_op jit(solution)/shard_map/pallas_call | solution.py:532

commit v5 on v4

--- a/solution.py
+++ b/solution.py
@@ -12,7 +12,7 @@
 MESH = pl.DeviceIdType.MESH
 QP = 256
 CAP = 4
-RELAYS = (2, 0)
+RELAYS = (3, 1)
 
 
 def dot_nn(a, b):
@@ -298,9 +298,9 @@
 
         own_copy(c).start()
 
+    prepare(0)
     copy_up.wait()
     turn_maps(up_in, up_maps, 8)
-    prepare(0)
     pl.semaphore_wait(barrier, expected)
 
     @functools.partial(repeat, chunks)
@@ -405,6 +405,21 @@
         out_v[c] = ost[...].reshape(q, wc, boxes).astype(BF)
         out_copy(c).start()
 
+    def settle(c):
+        @functools.partial(repeat, nbox - 1)
+        def _(j):
+            exchange(c, j + 1).wait_send()
+
+        for s in range(subs):
+            @pl.when(level > 0)
+            def _():
+                upward(c * subs + s).wait_send()
+
+        for r in range(len(relayed)):
+            @pl.when(carries[r])
+            def _():
+                carry_on(c, r).wait_send()
+
     @functools.partial(repeat, chunks)
     def _(c):
         near_field(c)
@@ -423,29 +438,24 @@
         own_copy(c).wait()
         far_field(c)
 
+        @pl.when(level >= nleaf // 2)
+        def _():
+            settle(c)
+
         for s in range(subs):
             descend(c, s)
         deliver(c)
 
+        @pl.when(level < nleaf // 2)
+        def _():
+            settle(c)
+
     @functools.partial(repeat, chunks)
     def _(c):
-        @functools.partial(repeat, nbox - 1)
-        def _(j):
-            exchange(c, j + 1).wait_send()
-
         for s in range(subs):
-            @pl.when(level > 0)
-            def _():
-                upward(c * subs + s).wait_send()
-
             @pl.when(level < last)
             def _():
                 downward(c * subs + s).wait_send()
-
-        for r in range(len(relayed)):
-            @pl.when(carries[r])
-            def _():
-                carry_on(c, r).wait_send()
 
         out_copy(c).wait()
 

time: 131 us -> 129 us (0.985)
  no operation moved by 1% of the time
where the time goes in v5:
time: 129 us
  Pallas kernels  129 us (100%)
    pallas_call x1, Pallas kernels, per_device(): pl.pallas_call(functools.partial(kernel, dims), out_shape=jax.ShapeDtypeS...  126 us
    pallas_call x1, Pallas kernels, per_device(): pl.pallas_call(functools.partial(copy_kernel, parts), out_shape=jax.Shape...  2.93 us

profile of v5, /device:TPU:31, one launch (start us, length us, event | category | flops | bytes accessed | tf_op | source)
XLA Modules:
  0.0 129.1 jit_solution(6587061211805639426)
XLA Ops:
  0.0 126.1 %shard_map.118.a_ref = bf16[216,64,128]{2,1,0:T(8,128)(2,1)} custom-call(bf16[216,64,128]{2,1,0:T(8,128)(2,1)} %bitcast.9, bf16[8,216,216]{2,1,0:T(8,128)(2,1)} %up_hbm.1, bf16[8,216,216]{2,1,0:T(8,128)(2,1)} %down_hbm.1, bf16[16,216,216]{2,1,0:T(8,128)(2,1)} %cross_hbm.1, s32[1,128]{1,0:T(1,128)} %octant_hbm.1, s32[1,128]{1,0:T(1,128)} %parent_hbm.1, ...), custom_call_target="tpu_custom_call" | custom-call | tf_op jit(solution)/shard_map/pallas_call | solution.py:496
  126.1 2.9 %shard_map.119 = bf16[216,64,128]{2,1,0:T(8,128)(2,1)} custom-call(bf16[216,64,128]{2,1,0:T(8,128)(2,1)} %shard_map.118.a_ref), custom_call_target="tpu_custom_call" | custom-call | tf_op jit(solution)/shard_map/pallas_call | solution.py:542

commit v6 on v5

--- a/solution.py
+++ b/solution.py
@@ -197,6 +197,9 @@
             recv_sem=sem_ar.at[c, j], device_id={"box": peer}, device_id_type=MESH,
         )
 
+    def in_chunk(c, r):
+        return jnp.asarray(c < chunks - 1) | (r < 2)
+
     def hand_over(c, r):
         to = lax.rem(me + relayed[r], nbox)
         return pltpu.make_async_remote_copy(
@@ -213,7 +216,7 @@
 
     def forward(c):
         for r in range(len(relayed)):
-            @pl.when(carries[r])
+            @pl.when(carries[r] & in_chunk(c, r))
             def _():
                 hand_over(c, r).wait_recv()
                 carry_on(c, r).start()
@@ -260,7 +263,7 @@
         def _(j):
             direct = j >= 0
             for r, offset in enumerate(relayed):
-                direct &= jnp.logical_not(hands_over[r] & (j + 1 == offset))
+                direct &= jnp.logical_not(hands_over[r] & in_chunk(c, r) & (j + 1 == offset))
 
             @pl.when(direct)
             def _():
@@ -288,7 +291,7 @@
             send[c, :, t * wc : (t + 1) * wc, :] = st[t].astype(BF).reshape(nbox, wc, 128)
 
         for r in range(len(relayed)):
-            @pl.when(hands_over[r])
+            @pl.when(hands_over[r] & in_chunk(c, r))
             def _():
                 hand_over(c, r).start()
 
@@ -323,7 +326,9 @@
     oh_near_slot = dot_nn(oh_slot, oh_near_dst).astype(BF)
     oh_far_slot = dot_nn(oh_slot, oh_far_dst).astype(BF)
     oh_bucket_t = oh_bucket.astype(F32).T.astype(BF)
-    oh_slot_bucket = dot_nn(oh_slot, oh_bucket_t).astype(BF)
+    slot_bucket = jnp.sum(oh_slot.astype(F32) * bucket_row.astype(F32), axis=1, keepdims=True)
+    pick_at = (iota((8 * par, par), 0) // par * par + iota((8 * par, par), 1)).astype(F32)
+    oh_pick = onehot(jnp.concatenate([slot_bucket] * 8, axis=0) == pick_at)
     copy_down.wait()
     turn_maps(down_in, down_maps, 8)
     copy_cross.wait()
@@ -383,20 +388,25 @@
         def _():
             downward(c * subs + s).wait_recv()
 
-        rows = ein[c * subs + s].reshape(ws * par, QP)
+        @pl.when(level < last)
+        def _():
+            for w in range(ws):
+                bucket[w] = dot_nn(oh_pick, ein[c * subs + s, w]).astype(BF)
+            rows = jnp.concatenate(
+                [bucket[:, o * par : (o + 1) * par, :].reshape(ws * par, QP) for o in range(8)], axis=1
+            )
+            total = dot_nn(rows, down_maps[...].reshape(8 * QP, QP))
+            held = far_slot[s * ws : (s + 1) * ws].reshape(ws * par, QP)
+            eout[c * subs + s] = (held + total).astype(BF).reshape(ws, par, QP)
+            downward(c * subs + s).start()
+
+    def deliver(c):
+        rows = ein[pl.ds(c * subs, subs)].reshape(wc * par, QP)
         for o in range(8):
-            shift[s * ws : (s + 1) * ws, o * par : (o + 1) * par, :] = (
-                dot_nn(rows, down_maps[o]).astype(BF).reshape(ws, par, QP)
+            shift[:, o * par : (o + 1) * par, :] = (
+                dot_nn(rows, down_maps[o]).astype(BF).reshape(wc, par, QP)
             )
-        for w in range(ws):
-            at = s * ws + w
-            eout[c * subs + s, w] = (far_slot[at] + dot_nn(oh_slot_bucket, shift[at])).astype(BF)
-
-        @pl.when(level < last)
-        def _():
-            downward(c * subs + s).start()
-
-    def deliver(c):
+
         @functools.partial(repeat, wc, unroll=8)
         def _(w):
             e_w = far[w] + dot_nn(oh_bucket_t, shift[w])
@@ -416,7 +426,7 @@
                 upward(c * subs + s).wait_send()
 
         for r in range(len(relayed)):
-            @pl.when(carries[r])
+            @pl.when(carries[r] & in_chunk(c, r))
             def _():
                 carry_on(c, r).wait_send()
 

time: 129 us -> 129 us (level); the launches traced: 129 us -> 127 us
  Pallas kernels: 129 us -> 127 us
    pallas_call x1, Pallas kernels: 126 us -> 124 us  [per_device(): pl.pallas_call(functools.partial(kernel, dims), out_shape=jax.ShapeDtypeS...]
where the time goes in v6:
time: 129 us; the launch traced here: 127 us
  Pallas kernels  127 us (98%)
    pallas_call x1, Pallas kernels, per_device(): pl.pallas_call(functools.partial(kernel, dims), out_shape=jax.ShapeDtypeS...  124 us
    pallas_call x1, Pallas kernels, per_device(): pl.pallas_call(functools.partial(copy_kernel, parts), out_shape=jax.Shape...  2.93 us

profile of v6, /device:TPU:31, one launch (start us, length us, event | category | flops | bytes accessed | tf_op | source)
XLA Modules:
  0.0 127.3 jit_solution(12408718171166507895)
XLA Ops:
  0.0 124.4 %shard_map.118.a_ref = bf16[216,64,128]{2,1,0:T(8,128)(2,1)} custom-call(bf16[216,64,128]{2,1,0:T(8,128)(2,1)} %bitcast.9, bf16[8,216,216]{2,1,0:T(8,128)(2,1)} %up_hbm.1, bf16[8,216,216]{2,1,0:T(8,128)(2,1)} %down_hbm.1, bf16[16,216,216]{2,1,0:T(8,128)(2,1)} %cross_hbm.1, s32[1,128]{1,0:T(1,128)} %octant_hbm.1, s32[1,128]{1,0:T(1,128)} %parent_hbm.1, ...), custom_call_target="tpu_custom_call" | custom-call | tf_op jit(solution)/shard_map/pallas_call | solution.py:506
  124.4 2.9 %shard_map.119 = bf16[216,64,128]{2,1,0:T(8,128)(2,1)} custom-call(bf16[216,64,128]{2,1,0:T(8,128)(2,1)} %shard_map.118.a_ref), custom_call_target="tpu_custom_call" | custom-call | tf_op jit(solution)/shard_map/pallas_call | solution.py:552
